TPU v7x, 128 devices: a whole 4x4x4 slice. The times are simulated.
128 devices in a mesh: dp: 8 (over x, core), fsdp: 16 (over y, z).
Axes of the slice: x: 4, y: 4, z: 4, core: 2. Of those that a mesh axis runs over, the one named last changes fastest.
Arguments:
- block_input: float32 [16384, 1024], P(('dp', 'fsdp')), may hold values from -6 to 6
- counts: int32 [8, 16], replicated, may hold values from 1 to 128, as said below
- query_weight: float32 [1, 1024, 2048], P(None, ('dp', 'fsdp')), may hold values from -0.1875 to 0.1875
- key_matrix: float32 [1, 1024, 1024], P(None, ('dp', 'fsdp')), may hold values from -0.1875 to 0.1875
- value_matrix: float32 [1, 1024, 1024], P(None, ('dp', 'fsdp')), may hold values from -0.1875 to 0.1875
- out_weight: float32 [1, 2048, 1024], P(None, ('dp', 'fsdp')), may hold values from -2 to 2
- gate_weight: float32 [1, 1024, 3072], P(None, ('dp', 'fsdp')), may hold values from -0.1875 to 0.1875
- up_weight: float32 [1, 1024, 3072], P(None, ('dp', 'fsdp')), may hold values from -0.1875 to 0.1875
- down_weight: float32 [1, 3072, 1024], P(None, ('dp', 'fsdp')), may hold values from -0.109375 to 0.109375
- attn_gain: float32 [1, 1024], P(None, ('dp', 'fsdp')), may hold values from 0.25 to 1.75
- mlp_gain: float32 [1, 1024], P(None, ('dp', 'fsdp')), may hold values from 0.25 to 1.75
- query_gain: float32 [1, 128], P(None, ('dp', 'fsdp')), may hold values from 0.25 to 1.75
- key_gain: float32 [1, 128], P(None, ('dp', 'fsdp')), may hold values from 0.25 to 1.75
- cotangent: float32 [16384, 1024], P(('dp', 'fsdp')), may hold values from -6 to 6
Outputs:
- block_output: float32 [16384, 1024], P(('dp', 'fsdp'))
- input_grad: float32 [16384, 1024], P(('dp', 'fsdp'))
- query_weight_grad: float32 [1, 1024, 2048], P(None, ('dp', 'fsdp'))
- key_weight_grad: float32 [1, 1024, 1024], P(None, ('dp', 'fsdp'))
- value_weight_grad: float32 [1, 1024, 1024], P(None, ('dp', 'fsdp'))
- out_weight_grad: float32 [1, 2048, 1024], P(None, ('dp', 'fsdp'))
- gate_weight_grad: float32 [1, 1024, 3072], P(None, ('dp', 'fsdp'))
- up_weight_grad: float32 [1, 1024, 3072], P(None, ('dp', 'fsdp'))
- down_weight_grad: float32 [1, 3072, 1024], P(None, ('dp', 'fsdp'))
- attn_gain_grad: float32 [1, 1024], P(None, ('dp', 'fsdp'))
- mlp_gain_grad: float32 [1, 1024], P(None, ('dp', 'fsdp'))
- query_gain_grad: float32 [1, 128], P(None, ('dp', 'fsdp'))
- key_gain_gradient: float32 [1, 128], P(None, ('dp', 'fsdp'))
Inputs may be any that keep to these rules, and one draw needn't show every extreme that they name: counts[g, d] slots of device d of group g are filled, from its first slot on; the rest are padding. The filled slots of a group, in device order, form one sequence. Device 0 of every group is full.
All inputs are finite; a program needn't handle non-finite values.
Results may differ from a plain program's by a relative error of at most 0.03.
Values may be sent and summed in bfloat16 or wider, within the bound.
No kernel may reach another device: no remote copies, remote signals or barrier semaphores. Data moves between devices by JAX's collectives and lax.ppermute only.
A program may use at most 192 MiB of HBM per device.

v0:
```python
from functools import partial

import jax
import jax.numpy as jnp
from jax import lax
from jax.sharding import PartitionSpec as P

QUERY_HEADS = 16
KEY_VALUE_HEADS = 8
HEAD_SIZE = 128
DECODER_LAYERS = 1


EPSILON = 1e-06
ROPE_BASE = 1000000.0
BLOCKED_SCORE = -1e30


def norm_apply(values, gain_vec):
    return values * lax.rsqrt(jnp.mean(values * values, -1, keepdims=True) + EPSILON) * gain_vec


def rotate(values, token_positions):
    half_width = values.shape[-1] // 2
    inverse = ROPE_BASE ** (-(jnp.arange(half_width, dtype=jnp.float32) * 2.0 / values.shape[-1]))
    angles = token_positions.astype(jnp.float32)[:, None] * inverse[None, :]
    cosine = jnp.cos(angles)[:, None, :]
    sine_part = jnp.sin(angles)[:, None, :]
    first_half = values[..., :half_width]
    second_half = values[..., half_width:]
    return jnp.concatenate(
        [
            first_half * cosine - second_half * sine_part,
            second_half * cosine + first_half * sine_part,
        ],
        -1,
    )


def head_apply(projected, gain_vec, token_positions):
    shaped = projected.reshape(projected.shape[0], -1, gain_vec.shape[0])
    return rotate(norm_apply(shaped, gain_vec), token_positions)


def score_block(query_rows, key_block, query_pos, key_pos, key_live):
    raw_scores = jnp.einsum(
        "rhgd,khd->hgrk", query_rows, key_block, preferred_element_type=jnp.float32
    )
    allowed = (key_pos[None, :] <= query_pos[:, None]) & key_live[None, :]
    return jnp.where(allowed, raw_scores * HEAD_SIZE ** (-0.5), BLOCKED_SCORE)


def split_blocks(key_row_matrix, value_row_matrix, key_pos, key_live, block_length):
    count_of_blocks = key_row_matrix.shape[0] // block_length
    return (
        key_row_matrix.reshape(count_of_blocks, block_length, KEY_VALUE_HEADS, HEAD_SIZE),
        value_row_matrix.reshape(count_of_blocks, block_length, KEY_VALUE_HEADS, HEAD_SIZE),
        key_pos.reshape(count_of_blocks, block_length),
        key_live.reshape(count_of_blocks, block_length),
    )


def attention_forward(query_rows, blocks, query_pos):
    count_of_rows = query_rows.shape[0]
    query_groups = QUERY_HEADS // KEY_VALUE_HEADS

    def first_pass(carry, block_item):
        top_score, exp_total = carry
        key_block, value_block, key_pos, key_live = block_item
        scores = score_block(query_rows, key_block, query_pos, key_pos, key_live)
        new_top = jnp.maximum(top_score, jnp.max(scores, -1))
        exp_total = exp_total * jnp.exp(top_score - new_top) + jnp.sum(
            jnp.exp(scores - new_top[..., None]), -1
        )
        return ((new_top, exp_total), None)

    initial = (
        jnp.full((KEY_VALUE_HEADS, query_groups, count_of_rows), BLOCKED_SCORE, jnp.float32),
        jnp.zeros((KEY_VALUE_HEADS, query_groups, count_of_rows), jnp.float32),
    )
    (top_score, exp_total), unused = lax.scan(first_pass, initial, blocks)
    log_total = top_score + jnp.log(exp_total)

    def second_pass(mixed_acc, block_item):
        key_block, value_block, key_pos, key_live = block_item
        scores = score_block(query_rows, key_block, query_pos, key_pos, key_live)
        prob_block = jnp.exp(scores - log_total[..., None]).astype(jnp.bfloat16)
        return (
            mixed_acc
            + jnp.einsum(
                "hgrk,khd->rhgd", prob_block, value_block, preferred_element_type=jnp.float32
            ),
            None,
        )

    mixed_heads, unused = lax.scan(second_pass, jnp.zeros(query_rows.shape, jnp.float32), blocks)
    return (log_total, mixed_heads)


def attention_backward(query_rows, blocks, log_total, mixed_heads, grad_heads, query_pos):
    row_delta = jnp.einsum("rhgd,rhgd->hgr", grad_heads.astype(jnp.float32), mixed_heads)

    def one_pass(query_acc, block_item):
        key_block, value_block, key_pos, key_live = block_item
        scores = score_block(query_rows, key_block, query_pos, key_pos, key_live)
        prob_block = jnp.exp(scores - log_total[..., None])
        prob_grad = jnp.einsum(
            "rhgd,khd->hgrk", grad_heads, value_block, preferred_element_type=jnp.float32
        )
        score_grad = (
            HEAD_SIZE ** (-0.5) * (prob_block * (prob_grad - row_delta[..., None]))
        ).astype(jnp.bfloat16)
        query_acc = query_acc + jnp.einsum(
            "hgrk,khd->rhgd", score_grad, key_block, preferred_element_type=jnp.float32
        )
        key_part = jnp.einsum(
            "hgrk,rhgd->khd", score_grad, query_rows, preferred_element_type=jnp.float32
        )
        value_part = jnp.einsum(
            "hgrk,rhgd->khd",
            prob_block.astype(jnp.bfloat16),
            grad_heads,
            preferred_element_type=jnp.float32,
        )
        return (query_acc, (key_part, value_part))

    query_grad, (key_pieces_list, value_pieces_list) = lax.scan(
        one_pass, jnp.zeros(query_rows.shape, jnp.float32), blocks
    )
    count_of_slots = key_pieces_list.shape[0] * key_pieces_list.shape[1]
    return (
        query_grad,
        key_pieces_list.reshape(count_of_slots, KEY_VALUE_HEADS * HEAD_SIZE),
        value_pieces_list.reshape(count_of_slots, KEY_VALUE_HEADS * HEAD_SIZE),
    )


def fetch_forward(masters, layer_index):
    pieces = [master[layer_index].astype(jnp.bfloat16) for master in masters]
    return (
        lax.all_gather(pieces[0], ("dp", "fsdp"), axis=0, tiled=True),
        lax.all_gather(pieces[1], ("dp", "fsdp"), axis=0, tiled=True),
        lax.all_gather(pieces[2], ("dp", "fsdp"), axis=0, tiled=True),
        lax.all_gather(pieces[3], ("dp", "fsdp"), axis=0, tiled=True),
        lax.all_gather(pieces[4], ("dp", "fsdp"), axis=0, tiled=True),
        lax.all_gather(pieces[5], ("dp", "fsdp"), axis=0, tiled=True),
        lax.all_gather(pieces[6], ("dp", "fsdp"), axis=0, tiled=True),
        lax.all_gather(pieces[7], ("dp", "fsdp"), axis=0, tiled=True),
        lax.all_gather(pieces[8], ("dp", "fsdp"), axis=0, tiled=True),
        lax.all_gather(pieces[9], ("dp", "fsdp"), axis=0, tiled=True),
        lax.all_gather(pieces[10], ("dp", "fsdp"), axis=0, tiled=True),
    )


def fetch_backward(masters, layer_index):
    pieces = [master[layer_index].astype(jnp.bfloat16) for master in masters]
    return (
        lax.all_gather(pieces[0], ("dp", "fsdp"), axis=0, tiled=True),
        lax.all_gather(pieces[1], ("dp", "fsdp"), axis=0, tiled=True),
        lax.all_gather(pieces[2], ("dp", "fsdp"), axis=0, tiled=True),
        lax.all_gather(pieces[3], ("dp", "fsdp"), axis=0, tiled=True),
        lax.all_gather(pieces[4], ("dp", "fsdp"), axis=0, tiled=True),
        lax.all_gather(pieces[5], ("dp", "fsdp"), axis=0, tiled=True),
        lax.all_gather(pieces[6], ("dp", "fsdp"), axis=0, tiled=True),
        lax.all_gather(pieces[7], ("dp", "fsdp"), axis=0, tiled=True),
        lax.all_gather(pieces[8], ("dp", "fsdp"), axis=0, tiled=True),
        lax.all_gather(pieces[9], ("dp", "fsdp"), axis=0, tiled=True),
        lax.all_gather(pieces[10], ("dp", "fsdp"), axis=0, tiled=True),
    )


def layer_forward(hidden, weights, query_pos, key_pos, key_live, block_length):
    (
        query_weight,
        key_matrix,
        value_matrix,
        out_weight,
        gate_weight,
        up_weight,
        down_weight,
        attn_gain,
        mlp_gain,
        query_gain,
        key_gain,
    ) = weights
    count_of_rows = hidden.shape[0]
    query_groups = QUERY_HEADS // KEY_VALUE_HEADS
    normed = norm_apply(hidden, attn_gain.astype(jnp.float32)).astype(jnp.bfloat16)
    query_proj = jnp.dot(normed, query_weight, preferred_element_type=jnp.float32)
    key_proj = jnp.dot(normed, key_matrix, preferred_element_type=jnp.float32)
    value_heads = (
        jnp.dot(normed, value_matrix, preferred_element_type=jnp.float32)
        .astype(jnp.bfloat16)
        .reshape(count_of_rows, KEY_VALUE_HEADS, HEAD_SIZE)
    )
    query_rows = (
        head_apply(query_proj, query_gain.astype(jnp.float32), query_pos)
        .astype(jnp.bfloat16)
        .reshape(count_of_rows, KEY_VALUE_HEADS, query_groups, HEAD_SIZE)
    )
    key_heads = head_apply(key_proj, key_gain.astype(jnp.float32), query_pos).astype(jnp.bfloat16)
    key_row_matrix, value_row_matrix = (
        lax.all_gather(key_heads, "fsdp", axis=0, tiled=True),
        lax.all_gather(value_heads, "fsdp", axis=0, tiled=True),
    )
    blocks = split_blocks(key_row_matrix, value_row_matrix, key_pos, key_live, block_length)
    log_total, mixed_heads = attention_forward(query_rows, blocks, query_pos)
    mixed_flattened = mixed_heads.reshape(count_of_rows, QUERY_HEADS * HEAD_SIZE).astype(
        jnp.bfloat16
    )
    middle = hidden + jnp.dot(mixed_flattened, out_weight, preferred_element_type=jnp.float32)
    second_normed = norm_apply(middle, mlp_gain.astype(jnp.float32)).astype(jnp.bfloat16)
    gate_proj = jnp.dot(second_normed, gate_weight, preferred_element_type=jnp.float32)
    up_proj = jnp.dot(second_normed, up_weight, preferred_element_type=jnp.float32)
    inner_act = (gate_proj * jax.nn.sigmoid(gate_proj) * up_proj).astype(jnp.bfloat16)
    result = middle + jnp.dot(inner_act, down_weight, preferred_element_type=jnp.float32)
    kept = (
        hidden,
        normed,
        query_proj,
        key_proj,
        query_rows,
        blocks,
        log_total,
        mixed_heads,
        mixed_flattened,
        middle,
        second_normed,
        gate_proj,
        up_proj,
        inner_act,
    )
    return (result, kept)


def layer_backward(grad_out, weights, kept, query_pos):
    (
        query_weight,
        key_matrix,
        value_matrix,
        out_weight,
        gate_weight,
        up_weight,
        down_weight,
        attn_gain,
        mlp_gain,
        query_gain,
        key_gain,
    ) = weights
    (
        hidden,
        normed,
        query_proj,
        key_proj,
        query_rows,
        blocks,
        log_total,
        mixed_heads,
        mixed_flattened,
        middle,
        second_normed,
        gate_proj,
        up_proj,
        inner_act,
    ) = kept
    count_of_rows = grad_out.shape[0]
    query_groups = QUERY_HEADS // KEY_VALUE_HEADS
    branch_grad = grad_out.astype(jnp.bfloat16)
    down_grad = jnp.einsum("rf,rd->fd", inner_act, branch_grad, preferred_element_type=jnp.float32)
    grad_inner = jnp.einsum(
        "rd,fd->rf", branch_grad, down_weight, preferred_element_type=jnp.float32
    )
    sigmoid_gate = jax.nn.sigmoid(gate_proj)
    gate_low = (
        grad_inner * up_proj * sigmoid_gate * (1.0 + gate_proj * (1.0 - sigmoid_gate))
    ).astype(jnp.bfloat16)
    up_low = (grad_inner * gate_proj * sigmoid_gate).astype(jnp.bfloat16)
    gate_grad = jnp.einsum("rd,rf->df", second_normed, gate_low, preferred_element_type=jnp.float32)
    up_grad = jnp.einsum("rd,rf->df", second_normed, up_low, preferred_element_type=jnp.float32)
    normed_grad = jnp.einsum(
        "rf,df->rd", gate_low, gate_weight, preferred_element_type=jnp.float32
    ) + jnp.einsum("rf,df->rd", up_low, up_weight, preferred_element_type=jnp.float32)
    unused, mlp_pull = jax.vjp(norm_apply, middle, mlp_gain.astype(jnp.float32))
    middle_part, mlp_gain_grad = mlp_pull(normed_grad)
    middle_grad = grad_out + middle_part
    attn_grad = middle_grad.astype(jnp.bfloat16)
    out_grad = jnp.einsum(
        "rc,rd->cd", mixed_flattened, attn_grad, preferred_element_type=jnp.float32
    )
    grad_heads = (
        jnp.einsum("rd,cd->rc", attn_grad, out_weight, preferred_element_type=jnp.float32)
        .astype(jnp.bfloat16)
        .reshape(count_of_rows, KEY_VALUE_HEADS, query_groups, HEAD_SIZE)
    )
    query_grad, key_partial, value_partial = attention_backward(
        query_rows, blocks, log_total, mixed_heads, grad_heads, query_pos
    )
    key_gradient, value_grad = (
        lax.psum_scatter(
            key_partial.astype(jnp.bfloat16), "fsdp", scatter_dimension=0, tiled=True
        ).astype(jnp.float32),
        lax.psum_scatter(
            value_partial.astype(jnp.bfloat16), "fsdp", scatter_dimension=0, tiled=True
        ).astype(jnp.float32),
    )
    unused, query_pull = jax.vjp(
        partial(head_apply, token_positions=query_pos), query_proj, query_gain.astype(jnp.float32)
    )
    query_proj_grad, query_gain_grad = query_pull(
        query_grad.reshape(count_of_rows, QUERY_HEADS, HEAD_SIZE)
    )
    unused, key_pullback = jax.vjp(
        partial(head_apply, token_positions=query_pos), key_proj, key_gain.astype(jnp.float32)
    )
    key_projection_gradient, key_gain_gradient = key_pullback(
        key_gradient.reshape(count_of_rows, KEY_VALUE_HEADS, HEAD_SIZE)
    )
    query_low = query_proj_grad.astype(jnp.bfloat16)
    key_low = key_projection_gradient.astype(jnp.bfloat16)
    value_low = value_grad.astype(jnp.bfloat16)
    query_w_grad = jnp.einsum("rd,rc->dc", normed, query_low, preferred_element_type=jnp.float32)
    key_w_grad = jnp.einsum("rd,rc->dc", normed, key_low, preferred_element_type=jnp.float32)
    value_w_grad = jnp.einsum("rd,rc->dc", normed, value_low, preferred_element_type=jnp.float32)
    input_part = jnp.einsum(
        "rc,dc->rd", query_low, query_weight, preferred_element_type=jnp.float32
    )
    input_part = input_part + jnp.einsum(
        "rc,dc->rd", key_low, key_matrix, preferred_element_type=jnp.float32
    )
    input_part = input_part + jnp.einsum(
        "rc,dc->rd", value_low, value_matrix, preferred_element_type=jnp.float32
    )
    unused, attn_pull = jax.vjp(norm_apply, hidden, attn_gain.astype(jnp.float32))
    hidden_part, attn_gain_grad = attn_pull(input_part)
    layer_grads = (
        query_w_grad,
        key_w_grad,
        value_w_grad,
        out_grad,
        gate_grad,
        up_grad,
        down_grad,
        attn_gain_grad,
        mlp_gain_grad,
        query_gain_grad,
        key_gain_gradient,
    )
    return (middle_grad + hidden_part, layer_grads)


def shards(
    block_input,
    counts,
    query_weight,
    key_matrix,
    value_matrix,
    out_weight,
    gate_weight,
    up_weight,
    down_weight,
    attn_gain,
    mlp_gain,
    query_gain,
    key_gain,
    cotangent,
):
    count_of_rows = block_input.shape[0]
    count_of_slots = count_of_rows * lax.axis_size("fsdp")
    block_length = min(512, count_of_slots)
    group_counts = lax.dynamic_index_in_dim(counts, lax.axis_index("dp"), 0, keepdims=False)
    member_index = lax.axis_index("fsdp")
    starts = jnp.cumsum(group_counts) - group_counts
    offsets = jnp.arange(count_of_rows, dtype=jnp.int32)
    key_pos = (starts[:, None] + offsets[None, :]).reshape(count_of_slots)
    key_live = (offsets[None, :] < group_counts[:, None]).reshape(count_of_slots)
    query_pos = lax.dynamic_index_in_dim(starts, member_index, 0, keepdims=False) + offsets
    query_live = offsets < lax.dynamic_index_in_dim(group_counts, member_index, 0, keepdims=False)
    masters = (
        query_weight,
        key_matrix,
        value_matrix,
        out_weight,
        gate_weight,
        up_weight,
        down_weight,
        attn_gain,
        mlp_gain,
        query_gain,
        key_gain,
    )
    hidden = block_input
    fetched_layers = []
    layer_index = 0
    weights = fetch_forward(masters, layer_index)
    hidden, kept = layer_forward(hidden, weights, query_pos, key_pos, key_live, block_length)
    kept_layers = [kept]
    fetched_layers.append(weights)
    grad_stream = cotangent * query_live[:, None].astype(jnp.float32)
    shares = [None] * DECODER_LAYERS
    for layer_index in reversed(range(DECODER_LAYERS)):
        weights = fetch_backward(masters, layer_index)
        grad_stream, layer_grads = layer_backward(
            grad_stream, weights, kept_layers[layer_index], query_pos
        )
        shares[layer_index] = (
            lax.psum_scatter(layer_grads[0], ("dp", "fsdp"), scatter_dimension=0, tiled=True),
            lax.psum_scatter(layer_grads[1], ("dp", "fsdp"), scatter_dimension=0, tiled=True),
            lax.psum_scatter(layer_grads[2], ("dp", "fsdp"), scatter_dimension=0, tiled=True),
            lax.psum_scatter(layer_grads[3], ("dp", "fsdp"), scatter_dimension=0, tiled=True),
            lax.psum_scatter(layer_grads[4], ("dp", "fsdp"), scatter_dimension=0, tiled=True),
            lax.psum_scatter(layer_grads[5], ("dp", "fsdp"), scatter_dimension=0, tiled=True),
            lax.psum_scatter(layer_grads[6], ("dp", "fsdp"), scatter_dimension=0, tiled=True),
            lax.psum_scatter(layer_grads[7], ("dp", "fsdp"), scatter_dimension=0, tiled=True),
            lax.psum_scatter(layer_grads[8], ("dp", "fsdp"), scatter_dimension=0, tiled=True),
            lax.psum_scatter(layer_grads[9], ("dp", "fsdp"), scatter_dimension=0, tiled=True),
            lax.psum_scatter(layer_grads[10], ("dp", "fsdp"), scatter_dimension=0, tiled=True),
        )
    stacked = [jnp.stack([shares[0][member]]) for member in range(11)]
    return (
        hidden,
        grad_stream,
        stacked[0],
        stacked[1],
        stacked[2],
        stacked[3],
        stacked[4],
        stacked[5],
        stacked[6],
        stacked[7],
        stacked[8],
        stacked[9],
        stacked[10],
    )


def solution(mesh):
    return jax.shard_map(
        shards,
        mesh=mesh,
        in_specs=(
            P(("dp", "fsdp"), None),
            P(),
            P(None, ("dp", "fsdp"), None),
            P(None, ("dp", "fsdp"), None),
            P(None, ("dp", "fsdp"), None),
            P(None, ("dp", "fsdp"), None),
            P(None, ("dp", "fsdp"), None),
            P(None, ("dp", "fsdp"), None),
            P(None, ("dp", "fsdp"), None),
            P(None, ("dp", "fsdp")),
            P(None, ("dp", "fsdp")),
            P(None, ("dp", "fsdp")),
            P(None, ("dp", "fsdp")),
            P(("dp", "fsdp"), None),
        ),
        out_specs=(
            P(("dp", "fsdp"), None),
            P(("dp", "fsdp"), None),
            P(None, ("dp", "fsdp"), None),
            P(None, ("dp", "fsdp"), None),
            P(None, ("dp", "fsdp"), None),
            P(None, ("dp", "fsdp"), None),
            P(None, ("dp", "fsdp"), None),
            P(None, ("dp", "fsdp"), None),
            P(None, ("dp", "fsdp"), None),
            P(None, ("dp", "fsdp")),
            P(None, ("dp", "fsdp")),
            P(None, ("dp", "fsdp")),
            P(None, ("dp", "fsdp")),
        ),
        check_vma=False,
    )
```

profile of v0, /device:TPU:0, one launch (start us, length us, event | category | flops | bytes accessed | tf_op | source)
XLA Modules:
  0.0 4110.8 jit_solution(13429450121534502807)
XLA Ops:
  14.9 69.5 %all-reduce.13 = (bf16[1024]{0:T(1024)(128)(2,1)S(1)}, bf16[128]{0:T(256)(128)(2,1)S(1)}, bf16[128]{0:T(256)(128)(2,1)S(1)}, bf16[1024]{0:T(1024)(128)(2,1)S(1)}) all-reduce(bf16[1024]{0:T(1024)(128)(2,1)S(1)} %dynamic-update-slice, bf16[128]{0:T(256)(128)(2,1)S(1)} %dynamic-update-slice.1, ...), channel_id=2, replica_groups=mesh['dp'=8,'fsdp'=16] {'dp','fsdp'}, use_global_device_ids=true, to_apply=%add.4 | all-reduce | flops 2304 | bytes 9216
  94.2 51.2 %all-gather.25.cloned.1.call-done = bf16[1,1024,1024]{2,1,0:T(8,128)(2,1)} async-done(((bf16[1,8,1024]{2,1,0:T(8,128)(2,1)}), bf16[1,1024,1024]{2,1,0:T(8,128)(2,1)}) %all-gather.25.cloned.1.call-update) | async-done | bytes 2097168 | tf_op jit(solution)/shard_map/all_gather | solution.py:143
  155.1 58.4 %all-gather.29.cloned.1.call-done = bf16[1,1024,2048]{2,1,0:T(8,128)(2,1)} async-done(((bf16[1,8,2048]{2,1,0:T(8,128)(2,1)}), bf16[1,1024,2048]{2,1,0:T(8,128)(2,1)}) %all-gather.29.cloned.1.call-update) | async-done | bytes 4194320 | tf_op jit(solution)/shard_map/all_gather | solution.py:141
  219.8 45.5 %all-gather.23.cloned.1.call-done = bf16[2048,8,128]{2,1,0:T(8,128)(2,1)} async-done(((bf16[128,8,128]{2,1,0:T(8,128)(2,1)}), bf16[2048,8,128]{2,1,0:T(8,128)(2,1)}) %all-gather.23.cloned.1.call-update) | async-done | bytes 4194320 | tf_op jit(solution)/shard_map/all_gather | solution.py:203
  270.5 35.1 while.39
  306.2 13.0 all-gather.21.cloned.1.call-done
  319.1 32.9 while.40
  353.3 35.8 all-gather.31.cloned.1.call-done
  392.4 66.0 %all-gather.35.cloned.1.call-done = bf16[1,1024,3072]{2,1,0:T(8,128)(2,1)} async-done(((bf16[1,8,3072]{2,1,0:T(8,128)(2,1)}), bf16[1,1024,3072]{2,1,0:T(8,128)(2,1)}) %all-gather.35.cloned.1.call-update) | async-done | bytes 6291472 | tf_op jit(solution)/shard_map/all_gather | solution.py:146
  463.4 64.5 %all-gather.37.cloned.1.call-done = bf16[1,3072,1024]{2,1,0:T(8,128)(2,1)} async-done(((bf16[1,24,1024]{2,1,0:T(8,128)(2,1)}), bf16[1,3072,1024]{2,1,0:T(8,128)(2,1)}) %all-gather.37.cloned.1.call-update) | async-done | bytes 6291472 | tf_op jit(solution)/shard_map/all_gather | solution.py:147
  534.1 62.8 %all-gather.33.cloned.1.call-done = bf16[1,1024,3072]{2,1,0:T(8,128)(2,1)} async-done(((bf16[1,8,3072]{2,1,0:T(8,128)(2,1)}), bf16[1,1024,3072]{2,1,0:T(8,128)(2,1)}) %all-gather.33.cloned.1.call-update) | async-done | bytes 6291472 | tf_op jit(solution)/shard_map/all_gather | solution.py:145
  622.4 59.4 %while.41 = (s32[]{:T(128)}, f32[128,8,2,128]{0,3,2,1:T(8,128)}, bf16[4,512,8,128]{3,1,2,0:T(8,128)(2,1)}, bf16[4,512,8,128]{3,1,2,0:T(8,128)(2,1)}, bf16[4,512,...) while((s32[]{:T(128)}, f32[128,8,2,128]{0,3,2,1:T(8,128)}, ...), condition=%wide.region_13.14_spmd.clone, body=%wide.region_12.13_spmd.clone.sunk | while | flops 1354367104 | bytes 104662008 | solution.py:127
  713.6 51.9 %reduce-scatter.10.cloned.1.call-done = bf16[128,1024]{1,0:T(8,128)(2,1)} async-done(((bf16[2048,1024]{1,0:T(8,128)(2,1)}), bf16[128,1024]{1,0:T(8,128)(2,1)}) %reduce-scatter.10.cloned.1.call-update) | async-done | bytes 262160 | tf_op jit(solution)/shard_map/reduce_scatter | solution.py:299
  771.0 75.4 %reduce-scatter.12.cloned.1.call-done = bf16[128,1024]{1,0:T(8,128)(2,1)} async-done(((bf16[2048,1024]{1,0:T(8,128)(2,1)}), bf16[128,1024]{1,0:T(8,128)(2,1)}) %reduce-scatter.12.cloned.1.call-update) | async-done | bytes 262160 | tf_op jit(solution)/shard_map/reduce_scatter | solution.py:302
  856.0 6.4 fusion.136
  871.1 6.5 fusion.133
  887.7 65.7 %all-reduce.12 = (f32[1024]{0:T(1024)S(1)}, f32[1024]{0:T(1024)S(1)}, f32[128]{0:T(128)S(1)}, f32[128]{0:T(128)S(1)}) all-reduce(f32[1024]{0:T(1024)S(1)} %get-tuple-element.434, f32[1024]{0:T(1024)S(1)} %copy-done.54, f32[128]{0:T(128)S(1)} %get-tuple-element.428, ...), channel_id=22, replica_groups=mesh['dp'=8,'fsdp'=16] {'dp','fsdp'}, use_global_device_ids=true, to_apply=%region_27.28.clone | all-reduce | flops 2304 | bytes 18432
  956.2 545.0 %reduce-scatter.14.cloned.1.call-done = f32[8,2048]{1,0:T(8,128)} async-done(((f32[1024,2048]{1,0:T(8,128)}), f32[8,2048]{1,0:T(8,128)}) %reduce-scatter.14.cloned.1.call-update) | async-done | bytes 65552 | tf_op jit(solution)/shard_map/reduce_scatter | solution.py:406
  1501.2 642.0 %reduce-scatter.16.cloned.1.call-done = f32[8,1024]{1,0:T(8,128)} async-done(((f32[1024,1024]{1,0:T(8,128)}), f32[8,1024]{1,0:T(8,128)}) %reduce-scatter.16.cloned.1.call-update) | async-done | bytes 32784 | tf_op jit(solution)/shard_map/reduce_scatter | solution.py:407
  2143.2 641.6 %reduce-scatter.18.cloned.1.call-done = f32[8,1024]{1,0:T(8,128)} async-done(((f32[1024,1024]{1,0:T(8,128)}), f32[8,1024]{1,0:T(8,128)}) %reduce-scatter.18.cloned.1.call-update) | async-done | bytes 32784 | tf_op jit(solution)/shard_map/reduce_scatter | solution.py:408
  2784.8 648.2 %reduce-scatter.20.cloned.1.call-done = f32[16,1024]{1,0:T(8,128)} async-done(((f32[2048,1024]{1,0:T(8,128)}), f32[16,1024]{1,0:T(8,128)}) %reduce-scatter.20.cloned.1.call-update) | async-done | bytes 65552 | tf_op jit(solution)/shard_map/reduce_scatter | solution.py:409
  3433.0 221.5 %reduce-scatter.22.cloned.1.call-done = f32[8,3072]{1,0:T(8,128)} async-done(((f32[1024,3072]{1,0:T(8,128)}), f32[8,3072]{1,0:T(8,128)}) %reduce-scatter.22.cloned.1.call-update) | async-done | bytes 98320 | tf_op jit(solution)/shard_map/reduce_scatter | solution.py:410
  3654.5 224.6 %reduce-scatter.24.cloned.1.call-done = f32[8,3072]{1,0:T(8,128)} async-done(((f32[1024,3072]{1,0:T(8,128)}), f32[8,3072]{1,0:T(8,128)}) %reduce-scatter.24.cloned.1.call-update) | async-done | bytes 98320 | tf_op jit(solution)/shard_map/reduce_scatter | solution.py:411
  3879.1 224.6 %reduce-scatter.26.cloned.1.call-done = f32[24,1024]{1,0:T(8,128)} async-done(((f32[3072,1024]{1,0:T(8,128)}), f32[24,1024]{1,0:T(8,128)}) %reduce-scatter.26.cloned.1.call-update) | async-done | bytes 98320 | tf_op jit(solution)/shard_map/reduce_scatter | solution.py:412
  (476 shorter events, 272.3 us)
Async XLA Ops:
  7.2 82.8 %all-gather.27.cloned.1.call-start = ((), (), s32[]{:S(2)}) async-start(), calls=%async_computation.21 | async-start | bytes 2113536 | tf_op jit(solution)/shard_map/all_gather | solution.py:142
  8.6 136.9 %all-gather.25.cloned.1.call-start = ((), (), s32[]{:S(2)}) async-start(), calls=%async_computation.20 | async-start | bytes 2113536 | tf_op jit(solution)/shard_map/all_gather | solution.py:143
  10.1 203.5 %all-gather.29.cloned.1.call-start = ((), (), s32[]{:S(2)}) async-start(), calls=%async_computation.22 | async-start | bytes 4227072 | tf_op jit(solution)/shard_map/all_gather | solution.py:141
  11.6 253.7 %all-gather.23.cloned.1.call-start = ((), (), s32[]{:S(2)}) async-start(), calls=%async_computation.10 | async-start | bytes 4456448 | tf_op jit(solution)/shard_map/all_gather | solution.py:203
  92.6 121.0 %copy-start.38 = (f32[128,8]{1,0:T(8,128)}, f32[128,8]{1,0:T(8,128)S(1)}, u32[]{:S(2)}) copy-start(f32[128,8]{1,0:T(8,128)S(1)} %copy.94) | copy-start | bytes 12292
  94.2 224.9 %all-gather.21.cloned.1.call-start = ((), (), s32[]{:S(2)}) async-start(), calls=%async_computation.9 | async-start | bytes 4456448 | tf_op jit(solution)/shard_map/all_gather | solution.py:204
  148.3 240.8 %all-gather.31.cloned.1.call-start = ((), (), s32[]{:S(2)}) async-start(), calls=%async_computation.23 | async-start | bytes 4227072 | tf_op jit(solution)/shard_map/all_gather | solution.py:144
  149.0 309.5 %all-gather.35.cloned.1.call-start = ((), (), s32[]{:S(2)}) async-start(), calls=%async_computation.25 | async-start | bytes 6340608 | tf_op jit(solution)/shard_map/all_gather | solution.py:146
  149.8 378.2 %all-gather.37.cloned.1.call-start = ((), (), s32[]{:S(2)}) async-start(), calls=%async_computation.26 | async-start | bytes 6340608 | tf_op jit(solution)/shard_map/all_gather | solution.py:147
  150.5 446.4 %all-gather.33.cloned.1.call-start = ((), (), s32[]{:S(2)}) async-start(), calls=%async_computation.24 | async-start | bytes 6340608 | tf_op jit(solution)/shard_map/all_gather | solution.py:145
  151.3 614.3 %reduce-scatter.10.cloned.1.call-start = ((), (), s32[]{:S(2)}) async-start(), calls=%async_computation.11 | async-start | bytes 4456448 | tf_op jit(solution)/shard_map/reduce_scatter | solution.py:299
  353.3 110.1 %copy-start.15 = (bf16[128,8,2,128]{0,3,2,1:T(8,128)(2,1)}, bf16[128,8,2,128]{0,3,2,1:T(8,128)(2,1)S(1)}, u32[]{:S(2)}) copy-start(bf16[128,8,2,128]{0,3,2,1:T(8,128)(2,1)S(1)} %convert_element_type.202) | copy-start | bytes 1572868
  392.3 219.6 %copy-start.8 = (f32[128,1024]{1,0:T(8,128)}, f32[128,1024]{1,0:T(8,128)S(1)}, u32[]{:S(2)}) copy-start(f32[128,1024]{1,0:T(8,128)S(1)} %get-tuple-element.524) | copy-start | bytes 1572868
  392.4 204.5 %copy-start.18 = (bf16[128,1024]{1,0:T(8,128)(2,1)}, bf16[128,1024]{1,0:T(8,128)(2,1)S(1)}, u32[]{:S(2)}) copy-start(bf16[128,1024]{1,0:T(8,128)(2,1)S(1)} %multiply_convert_fusion.3) | copy-start | bytes 786436
  392.4 135.6 %copy-start.22 = (f32[128,1024]{1,0:T(8,128)S(1)}, f32[128,1024]{1,0:T(8,128)}, u32[]{:S(2)}) copy-start(f32[128,1024]{1,0:T(8,128)} %param.33) | copy-start | bytes 1572868
  392.4 135.6 %copy-start.59 = (f32[128]{0:T(128)S(1)}, f32[128]{0:T(128)}, u32[]{:S(2)}) copy-start(f32[128]{0:T(128)} %compare_convert_fusion) | copy-start | bytes 1540
  689.9 156.5 %reduce-scatter.12.cloned.1.call-start = ((), (), s32[]{:S(2)}) async-start(), calls=%async_computation.12 | async-start | bytes 4456448 | tf_op jit(solution)/shard_map/reduce_scatter | solution.py:302
  698.2 803.0 %reduce-scatter.14.cloned.1.call-start = ((), (), s32[]{:S(2)}) async-start(), calls=%async_computation.13 | async-start | bytes 8454144 | tf_op jit(solution)/shard_map/reduce_scatter | solution.py:406
  713.5 1429.6 %reduce-scatter.16.cloned.1.call-start = ((), (), s32[]{:S(2)}) async-start(), calls=%async_computation.14 | async-start | bytes 4227072 | tf_op jit(solution)/shard_map/reduce_scatter | solution.py:407
  770.9 2013.9 %reduce-scatter.18.cloned.1.call-start = ((), (), s32[]{:S(2)}) async-start(), calls=%async_computation.15 | async-start | bytes 4227072 | tf_op jit(solution)/shard_map/reduce_scatter | solution.py:408
  850.1 2582.9 %reduce-scatter.20.cloned.1.call-start = ((), (), s32[]{:S(2)}) async-start(), calls=%async_computation.16 | async-start | bytes 8454144 | tf_op jit(solution)/shard_map/reduce_scatter | solution.py:409
  854.8 2799.7 %reduce-scatter.22.cloned.1.call-start = ((), (), s32[]{:S(2)}) async-start(), calls=%async_computation.17 | async-start | bytes 12681216 | tf_op jit(solution)/shard_map/reduce_scatter | solution.py:410
  862.4 3016.7 %reduce-scatter.24.cloned.1.call-start = ((), (), s32[]{:S(2)}) async-start(), calls=%async_computation.18 | async-start | bytes 12681216 | tf_op jit(solution)/shard_map/reduce_scatter | solution.py:411
  869.8 3233.9 %reduce-scatter.26.cloned.1.call-start = ((), (), s32[]{:S(2)}) async-start(), calls=%async_computation.19 | async-start | bytes 12681216 | tf_op jit(solution)/shard_map/reduce_scatter | solution.py:412
  (99 other events, 1033.0 us)
Sparse Core Ops, SparseCore 0:
  11.6 67.7 all-gather.26
  82.9 62.5 all-gather.24
  149.2 64.2 all-gather.28
  216.1 49.1 all-gather.22
  267.8 51.2 all-gather.20
  322.7 66.4 all-gather.30
  392.8 65.6 all-gather.34
  462.1 65.8 all-gather.36
  531.1 65.8 all-gather.32
  690.0 75.4 reduce-scatter.9
  769.2 77.0 reduce-scatter.11
  849.1 651.9 reduce-scatter.13
  1504.2 638.8 reduce-scatter.15
  2145.9 638.8 reduce-scatter.17
  2787.7 645.2 reduce-scatter.19
  3438.4 216.0 reduce-scatter.21
  3659.9 219.1 reduce-scatter.23
  3884.5 219.1 reduce-scatter.25
where the time goes:
time: 4120 us; the launch traced here: 4110 us
  waiting for transfers between devices  3670 us (89%)
  matrix products  151 us (4%)
  blocking collectives  135 us (3%)
  local copies, waits for them, and re-layouts  75.9 us (2%)
  other arithmetic  56 us (1%)
    reduce_scatter x1, waiting for transfers between devices, shards(): lax.psum_scatter(layer_grads[3], ('dp', 'fsdp'), scatter_dimension=0, til...  648 us
    reduce_scatter x1, waiting for transfers between devices, shards(): lax.psum_scatter(layer_grads[1], ('dp', 'fsdp'), scatter_dimension=0, til...  642 us
    reduce_scatter x1, waiting for transfers between devices, shards(): lax.psum_scatter(layer_grads[2], ('dp', 'fsdp'), scatter_dimension=0, til...  642 us
    reduce_scatter x1, waiting for transfers between devices, shards(): lax.psum_scatter(layer_grads[0], ('dp', 'fsdp'), scatter_dimension=0, til...  545 us
    reduce_scatter x1, waiting for transfers between devices, shards(): lax.psum_scatter(layer_grads[6], ('dp', 'fsdp'), scatter_dimension=0, til...  225 us
    reduce_scatter x1, waiting for transfers between devices, shards(): lax.psum_scatter(layer_grads[5], ('dp', 'fsdp'), scatter_dimension=0, til...  225 us
    reduce_scatter x1, waiting for transfers between devices, shards(): lax.psum_scatter(layer_grads[4], ('dp', 'fsdp'), scatter_dimension=0, til...  221 us
    unnamed x2, blocking collectives  135 us
  transfers between devices with their start and end apart: 18, of which 17 were waited for; matrix products, arithmetic and copies ran while one was open for 4% of the time, Pallas kernels for 0%

commit v1 on v0

v1 whole, which is shorter than its diff:
```python
import functools

import jax
import jax.numpy as jnp
from jax import lax
from jax.experimental import pallas as pl
from jax.experimental.pallas import tpu as pltpu
from jax.sharding import Mesh, PartitionSpec as P

HEADS = 16
KV_HEADS = 8
SIZE = 128
WIDTH = 1024
ROWS = 128
PLACES = 16
EPSILON = 1e-06
ROPE_BASE = 1000000.0
SCALE = SIZE**-0.5
SCALE2 = SCALE * 1.4426950408889634
F32 = jnp.float32
BF16 = jnp.bfloat16
MIB = 1 << 20

TOKENS = ("y", "z")
ALL = ("x", "core", "y", "z")

UNITS = 11
HALVES = [(u, c) for u in range(UNITS) for c in range(2)]
PARTS = [HALVES[:11], HALVES[11:]]
ORDERS = (("x", "y"), ("y", "x"))
MASKS = ((1, 3), (3, 1))
KEPT = ((0, 3, 1, 2), (0, 1, 3, 2))
QUARTERS = [(p, m, h) for p in range(2) for m, h in enumerate((PARTS[p][:6], PARTS[p][6:]))]
PAIRS = [(0, 0), (1, 0)] + [(2, 1 + t) for t in range(6)] + [(3 + t, 7) for t in range(3)]


def matmul(a, b):
    return lax.dot_general(a, b, (((1,), (0,)), ((), ())), preferred_element_type=F32)


def matmul_nt(a, b):
    return lax.dot_general(a, b, (((1,), (1,)), ((), ())), preferred_element_type=F32)


def matmul_tn(a, b):
    return lax.dot_general(a, b, (((0,), (0,)), ((), ())), preferred_element_type=F32)


def exact(a, b):
    return lax.dot_general(
        a, b, (((1,), (0,)), ((), ())), preferred_element_type=F32, precision=lax.Precision.HIGHEST
    )


SMEM = pl.BlockSpec(memory_space=pltpu.SMEM)
HBM = pl.BlockSpec(memory_space=pltpu.HBM)


class Moves:
    def __init__(self, ins, outs, sems):
        self.ins, self.outs, self.sems, self.sent, self.pushed = ins, outs, sems, [], 0

    def need(self, *which):
        for i in which or list(self.ins):
            if i in self.ins:
                self.ins.pop(i).wait()

    def flush(self, *which):
        for i in which or list(self.outs):
            if i in self.outs:
                copy = self.outs.pop(i)
                copy.start()
                self.sent.append(copy)

    def push(self, source, target):
        copy = pltpu.make_async_copy(source, target, self.sems.at[self.pushed])
        copy.start()
        self.sent.append(copy)
        self.pushed += 1

    def finish(self):
        self.need()
        self.flush()
        for copy in self.sent:
            copy.wait()


def call(
    kernel, outs, args, scalars=(), anywhere=(), raw=(), scratch=(), limit=60, flops=0, nbytes=0, sends=0
):
    moved = [i for i in range(len(args)) if i not in scalars and i not in anywhere]
    made = [i for i in range(len(outs)) if i not in raw]
    count, total = len(args), len(outs)

    def body(*refs):
        ins, out, rest = list(refs[:count]), list(refs[count : count + total]), list(refs[count + total :])
        here = [rest.pop(0) for i in moved]
        there = [rest.pop(0) for i in made]
        sems_in, sems_out = rest.pop(0), rest.pop(0)
        copies_in = {i: pltpu.make_async_copy(ins[i], here[n], sems_in.at[n]) for n, i in enumerate(moved)}
        copies_out = {
            i: pltpu.make_async_copy(there[n], out[i], sems_out.at[sends + n]) for n, i in enumerate(made)
        }
        for copy in copies_in.values():
            copy.start()
        for n, i in enumerate(moved):
            ins[i] = here[n]
        for n, i in enumerate(made):
            out[i] = there[n]
        moves = Moves(copies_in, copies_out, sems_out)
        kernel(moves, *ins, *out, *rest)
        moves.finish()

    buffers = [pltpu.VMEM(args[i].shape, args[i].dtype) for i in moved]
    buffers += [pltpu.VMEM(*outs[i]) for i in made]
    sems = [pltpu.SemaphoreType.DMA((max(len(moved), 1),)), pltpu.SemaphoreType.DMA((len(made) + sends,))]
    return pl.pallas_call(
        body,
        out_shape=[jax.ShapeDtypeStruct(s, t) for s, t in outs],
        in_specs=[SMEM if i in scalars else HBM for i in range(count)],
        out_specs=[HBM] * total,
        scratch_shapes=buffers + sems + list(scratch),
        compiler_params=pltpu.CompilerParams(vmem_limit_bytes=limit * MIB),
        cost_estimate=pl.CostEstimate(flops=flops, bytes_accessed=nbytes, transcendentals=0),
    )(*args)


def iota(shape, dim):
    return lax.broadcasted_iota(jnp.int32, shape, dim)


def mean_scale(v):
    return lax.rsqrt(jnp.mean(v * v, -1, keepdims=True) + EPSILON)


def norm_back(grad, normal, scale):
    return scale * (grad - normal * jnp.mean(grad * normal, -1, keepdims=True))


def swap_halves(v):
    return pltpu.roll(v, 64, 1)


def column(row):
    return jnp.sum(jnp.where(iota((8, 8), 0) == iota((8, 8), 1), row, 0.0), 1, keepdims=True)


def hidden_map(back):
    shape = (384, 384)
    source, target = (iota(shape, 1), iota(shape, 0)) if back else (iota(shape, 0), iota(shape, 1))
    i, rest = source // 24, source % 24
    return jnp.where((rest // 8) * 128 + i * 8 + rest % 8 == target, 1.0, 0.0)


def channel_map(back):
    shape = (128, 128)
    source, target = (iota(shape, 1), iota(shape, 0)) if back else (iota(shape, 0), iota(shape, 1))
    i, rest = source // 16, source % 16
    return jnp.where((rest // 8) * 64 + i * 8 + rest % 8 == target, 1.0, 0.0)


def prepare_kernel(moves, x_ref, o_ref, g_ref, u_ref, d_ref, g2_ref, ff_ref, n0_ref, n1_ref):
    moves.need(0)
    x = x_ref[...]
    normal = (x * mean_scale(x)).astype(BF16)
    n0_ref[...] = normal[:, :512]
    n1_ref[...] = normal[:, 512:]
    moves.flush(1, 2)
    moves.need()
    gain2 = column(g2_ref[...].astype(BF16).astype(F32))
    for t in range(2):
        ff_ref[t] = o_ref[0, 8 * t : 8 * t + 8].astype(BF16)
    for t in range(3):
        ff_ref[8 + t] = d_ref[0, 8 * t : 8 * t + 8].astype(BF16)
    order = hidden_map(False).astype(BF16)
    for base, ref in ((2, g_ref), (5, u_ref)):
        w = (ref[0].astype(BF16).astype(F32) * gain2).astype(BF16).astype(F32)
        tall = jnp.concatenate([w[:, 384 * i : 384 * i + 384] for i in range(8)], 0).astype(BF16)
        tall = matmul(tall, order)
        for t in range(3):
            for i in range(8):
                ff_ref[base + t, :, 128 * i : 128 * i + 128] = tall[
                    8 * i : 8 * i + 8, 128 * t : 128 * t + 128
                ].astype(BF16)


def prepare(x, out_weight, gate, up, down, gain2):
    outs = [((UNITS, 8, WIDTH), BF16)] + [((ROWS, 512), BF16)] * 2
    return call(
        prepare_kernel, outs, (x, out_weight, gate, up, down, gain2), flops=10**7, nbytes=2 * MIB,
    )


def pack_heads_kernel(moves, own, gq_ref, gk_ref, q_ref, k_ref, v_ref, g1_ref, after, send_ref):
    moves.need()
    gain1 = column(g1_ref[...].astype(BF16).astype(F32))

    def scaled(ref):
        return (ref[0].astype(BF16).astype(F32) * gain1).astype(BF16)

    query = scaled(q_ref)
    key = scaled(k_ref)
    value = scaled(v_ref).astype(F32)
    value = jnp.concatenate([value[:, 128 * i : 128 * i + 128] for i in range(8)], 0).astype(BF16)
    value = matmul(value, channel_map(False).astype(BF16))
    spot = iota((8, SIZE), 1) == own[0]
    row = iota((8, SIZE), 0)
    gq = jnp.full((8, SIZE), gq_ref[0, 0], F32).astype(BF16).astype(F32)
    gk = jnp.full((8, SIZE), gk_ref[0, 0], F32).astype(BF16).astype(F32)
    gains = jnp.where(spot & (row == 0), gq, jnp.where(spot & (row == 1), gk, 0.0)).astype(BF16)
    for f in range(HEADS):
        h = f // 2
        tile = jnp.concatenate(
            [
                query[:, 128 * f : 128 * f + 128],
                key[:, 128 * h : 128 * h + 128],
                value[8 * h : 8 * h + 8].astype(BF16),
                gains,
            ],
            1,
        )
        send_ref[f] = tile


def pack_heads(own, gq, gk, q, k, v, g1, after):
    return call(
        pack_heads_kernel, [((HEADS, 8, 512), BF16)], (own, gq, gk, q, k, v, g1, after),
        scalars=(0, 1, 2), anywhere=(7,), flops=10**7, nbytes=2 * MIB,
    )[0]


def pack_rows_kernel(moves, q_ref, k_ref, v_ref, g1_ref, after, out_ref):
    moves.need()
    gain1 = column(g1_ref[...].astype(BF16).astype(F32))

    def scaled(w):
        return (w.astype(BF16).astype(F32) * gain1).astype(BF16)

    out_ref[0] = scaled(q_ref[0, :, :WIDTH])
    out_ref[1] = scaled(q_ref[0, :, WIDTH:])
    out_ref[2] = scaled(k_ref[0])
    value = scaled(v_ref[0]).astype(F32)
    value = jnp.concatenate([value[:, 128 * i : 128 * i + 128] for i in range(8)], 0).astype(BF16)
    value = matmul(value, channel_map(False).astype(BF16))
    for i in range(8):
        out_ref[3, :, 128 * i : 128 * i + 128] = value[8 * i : 8 * i + 8].astype(BF16)


def pack_rows(q, k, v, g1, after):
    return call(
        pack_rows_kernel, [((4, 8, WIDTH), BF16)], (q, k, v, g1, after), anywhere=(4,),
        flops=10**7, nbytes=MIB,
    )[0]


def row_limits(scal, first, shape, along):
    at = iota(shape, along)
    block, offset = at // ROWS, at % ROWS
    start = jnp.zeros(shape, jnp.int32)
    for i in range(4):
        start = jnp.where(block == i, scal[2 + first + i], start)
    return jnp.minimum(start + offset, scal[1] - 1)


def places(scal, part, late, early):
    first, second = scal[34 + part] ^ early, scal[35 - part] ^ late
    return 4 * first + second if part == 0 else 4 * second + first


def attend_kernel(moves, scal, *refs):
    tokens, (own_ref, other_ref, cos_ref, sin_ref) = (refs[:4], refs[4:8]), refs[8:12]
    o_ref, q_ref, k_ref, v_ref, lse_ref, p_ref, w_ref, kc, vc, va, acc, proj = refs[12:]
    total = scal[1]
    kc[...] = jnp.zeros_like(kc)
    vc[...] = jnp.zeros_like(vc)
    va[:, 128:] = jnp.ones((PLACES * ROWS, 128), BF16)
    moves.need(9, 10)
    for mask in range(4):
        for c, ref in enumerate((own_ref, other_ref)):
            block = 2 * (scal[36] ^ mask) + (scal[37] ^ c)
            w_ref[pl.ds(pl.multiple_of(ROWS * block, ROWS), ROWS), :] = ref[mask]
    moves.flush(6)
    for part in range(2):
        for late in range(4):
            moves.need(1 + 4 * part + late)
            w = w_ref[512 * part : 512 * part + 512, :384]
            out = matmul(tokens[part][late][...].reshape(4 * ROWS, 512), w)
            for early in range(4):
                e = places(scal, part, late, early)
                block = out[ROWS * early : ROWS * early + ROWS]
                if part == 0:
                    proj[e] = block
                else:
                    proj[e] += block
    moves.need()
    rows8 = iota((WIDTH, SIZE), 0) % 8
    gains = w_ref[:, 384:].astype(F32)
    query_gain = jnp.sum(jnp.where(rows8 == 0, gains, 0.0), 0, keepdims=True)
    key_gain = jnp.sum(jnp.where(rows8 == 1, gains, 0.0), 0, keepdims=True)
    for e in range(PLACES):
        block = proj[e]
        query, key = block[:, :128], block[:, 128:256]
        p_ref[e] = block[:, :256]
        cos, sin = cos_ref[e], sin_ref[e]
        query = query * mean_scale(query) * query_gain
        q_ref[e] = (query * cos + swap_halves(query) * sin).astype(BF16)
        key = key * mean_scale(key) * key_gain
        start = scal[2 + e]
        kc[pl.ds(start, ROWS), :] = key * cos + swap_halves(key) * sin
        vc[pl.ds(start, ROWS), :] = block[:, 256:]
    moves.flush(5)
    slots = PLACES * ROWS
    k_ref[...] = kc[:slots].astype(BF16)
    v_ref[...] = vc[:slots].astype(BF16)
    va[:, :128] = v_ref[...]
    moves.flush(1, 2, 3)

    for j in range(4):
        query = q_ref[4 * j : 4 * j + 4].reshape(512, SIZE)
        limit = row_limits(scal, 4 * j, (512, 512), 0)
        acc[...] = jnp.zeros_like(acc)

        def step(masked, query=query, limit=limit):
            def body(b, carry):
                at = pl.multiple_of(b * 512, 512)
                s = matmul_nt(query, k_ref[pl.ds(at, 512), :])
                prob = jnp.exp2(s * SCALE2)
                if masked:
                    prob = jnp.where(iota((512, 512), 1) + at <= limit, prob, 0.0)
                acc[...] += matmul(prob.astype(BF16), va[pl.ds(at, 512), :])
                return carry

            return body

        full = (scal[2 + 4 * j] + 1) // 512
        last = jnp.minimum(scal[2 + 4 * j + 3] + ROWS - 1, total - 1) // 512 + 1
        lax.fori_loop(0, full, step(False), 0)
        lax.fori_loop(full, last, step(True), 0)
        weight = acc[:, 128:]
        o_ref[4 * j : 4 * j + 4] = (
            (acc[:, :128] / weight).astype(BF16).reshape(4, ROWS, SIZE)
        )
        lse_ref[:, 512 * j : 512 * j + 512] = jnp.log2(weight).T[:8]


def attend(scal, tokens, weights, cos, sin):
    slots = PLACES * ROWS
    blocks = (PLACES, ROWS, SIZE)
    outs = [
        (blocks, BF16),
        (blocks, BF16),
        ((slots, SIZE), BF16),
        ((slots, SIZE), BF16),
        ((8, slots), F32),
        ((PLACES, ROWS, 256), F32),
        ((WIDTH, 512), BF16),
    ]
    scratch = [
        pltpu.VMEM((slots + ROWS, SIZE), F32),
        pltpu.VMEM((slots + ROWS, SIZE), F32),
        pltpu.VMEM((slots, 256), BF16),
        pltpu.VMEM((512, 256), F32),
        pltpu.VMEM((PLACES, ROWS, 384), F32),
    ]
    return call(
        attend_kernel, outs, (scal, *tokens, *weights, cos, sin), (0,), scratch=scratch,
        flops=5 * 10**9, nbytes=12 * MIB,
    )


def retreat_kernel(
    moves, scal, do_ref, o_ref, q_ref, k_ref, v_ref, lse_ref, after, dq, dk, dv, delta
):
    total = scal[1]
    moves.need()
    dk[...] = jnp.zeros_like(dk)
    dv[...] = jnp.zeros_like(dv)
    ones = jnp.ones((8, SIZE), F32)

    for j in range(4):
        query = q_ref[4 * j : 4 * j + 4].reshape(512, SIZE)
        grad = do_ref[4 * j : 4 * j + 4].reshape(512, SIZE)
        out = o_ref[4 * j : 4 * j + 4].reshape(512, SIZE)
        prod = grad.astype(F32) * out.astype(F32)
        delta[...] = lax.dot_general(
            ones, prod, (((1,), (1,)), ((), ())), preferred_element_type=F32,
            precision=lax.Precision.HIGHEST,
        )
        limit = row_limits(scal, 4 * j, (8, 512), 1)[:1]
        dq[j] = jnp.zeros((512, SIZE), F32)

        def step(masked, query=query, grad=grad, limit=limit, j=j):
            def body(b, carry):
                at = pl.multiple_of(b * 512, 512)
                key = k_ref[pl.ds(at, 512), :]
                s = matmul_nt(key, query)
                prob = jnp.exp2(s * SCALE2 - lse_ref[:1, 512 * j : 512 * j + 512])
                if masked:
                    prob = jnp.where(iota((512, 512), 0) + at <= limit, prob, 0.0)
                dv[pl.ds(at, 512), :] += matmul(prob.astype(BF16), grad)
                prob_grad = matmul_nt(v_ref[pl.ds(at, 512), :], grad)
                score = (prob * (prob_grad - delta[:1])).astype(BF16)
                dk[pl.ds(at, 512), :] += matmul(score, query)
                dq[j] += matmul_tn(score, key)
                return carry

            return body

        full = (scal[2 + 4 * j] + 1) // 512
        last = jnp.minimum(scal[2 + 4 * j + 3] + ROWS - 1, total - 1) // 512 + 1
        lax.fori_loop(0, full, step(False), 0)
        lax.fori_loop(full, last, step(True), 0)


def retreat(scal, head_grad, saved, after):
    outs = [((4, 512, SIZE), F32)] + [((PLACES * ROWS + ROWS, SIZE), F32)] * 2
    return call(
        retreat_kernel, outs, (scal, head_grad, *saved, after), (0,), (7,),
        scratch=[pltpu.VMEM((8, 512), F32)], flops=8 * 10**9, nbytes=6 * MIB,
    )


def project_kernel(
    moves, scal, w_ref, cos_ref, sin_ref, p_ref, dq, dk, dv, after, low, gains_ref
):
    moves.need()
    rows8 = iota((WIDTH, SIZE), 0) % 8
    gains = w_ref[:, 384:].astype(F32)
    query_gain = jnp.sum(jnp.where(rows8 == 0, gains, 0.0), 0, keepdims=True)
    key_gain = jnp.sum(jnp.where(rows8 == 1, gains, 0.0), 0, keepdims=True)

    query_part = jnp.zeros((1, SIZE), F32)
    key_part = jnp.zeros((1, SIZE), F32)

    def head(grad, projected, gain, cos, sin):
        turned = grad * cos - swap_halves(grad) * sin
        scale = mean_scale(projected)
        normal = projected * scale
        part = jnp.sum(turned * normal, 0, keepdims=True)
        return norm_back(turned * gain, normal, scale).astype(BF16), part

    for e in range(PLACES):
        cos, sin = cos_ref[e], sin_ref[e]
        at = ROWS * (e % 4)
        query_grad = dq[e // 4, at : at + ROWS, :] * SCALE
        low[e, :, :128], part = head(query_grad, p_ref[e, :, :128], query_gain, cos, sin)
        query_part += part
        live = iota((ROWS, SIZE), 0) < scal[18 + e]
        start = scal[2 + e]
        key_grad = jnp.where(live, dk[pl.ds(start, ROWS), :], 0.0) * SCALE
        low[e, :, 128:256], part = head(key_grad, p_ref[e, :, 128:], key_gain, cos, sin)
        key_part += part
        low[e, :, 256:] = jnp.where(live, dv[pl.ds(start, ROWS), :], 0.0).astype(BF16)

    gains_ref[...] = jnp.where(iota((8, SIZE), 0) == 0, query_part, key_part)


def project(scal, weight, cos, sin, projected, grads, after):
    outs = [((PLACES, ROWS, 384), BF16), ((8, SIZE), F32)]
    return call(
        project_kernel, outs, (scal, weight, cos, sin, projected, *grads, after), (0,), (8,),
        flops=10**8, nbytes=10 * MIB,
    )


def weigh_heads_kernel(moves, scal, *refs):
    tokens, (low, gains_ref, mine_ref, theirs_ref, grad) = (refs[:4], refs[4:8]), refs[8:]
    moves.need()
    for part in range(2):
        total = jnp.zeros((512, 384), F32)
        for late in range(4):
            rows = jnp.concatenate([low[places(scal, part, late, early)] for early in range(4)], 0)
            total += matmul_tn(tokens[part][late][...].reshape(4 * ROWS, 512), rows)
        grad[512 * part : 512 * part + 512, :384] = total.astype(BF16)
    rows8 = iota((WIDTH, SIZE), 0) % 8
    spot = iota((WIDTH, SIZE), 0) // 8 == iota((WIDTH, SIZE), 1)
    extra = jnp.where(rows8 == 0, gains_ref[:1], jnp.where(rows8 == 1, gains_ref[1:2], 0.0))
    grad[:, 384:] = jnp.where(spot, extra, 0.0).astype(BF16)
    for x in range(4):
        for c, ref in enumerate((mine_ref, theirs_ref)):
            block = 2 * x + (scal[37] ^ c)
            ref[x] = grad[pl.ds(pl.multiple_of(ROWS * block, ROWS), ROWS), :]


def weigh_heads(scal, tokens, low, gains):
    return call(
        weigh_heads_kernel, [((4, ROWS, 512), BF16)] * 2, (scal, *tokens, low, gains), (0,),
        scratch=[pltpu.VMEM((WIDTH, 512), BF16)], flops=2 * 10**9, nbytes=7 * MIB,
    )


def feed_kernel(
    moves, scal, mixed_ref, x_ref, cot_ref, ff_ref,
    out_ref, mg_ref, send_ref, mine_ref, theirs_ref, right_ref,
    w, sems, gate, up, half, normal,
):
    core, count = scal[0], scal[1]
    copies = [pltpu.make_async_copy(ff_ref.at[u], w.at[u], sems.at[u]) for u in range(UNITS)]
    for copy in copies:
        copy.start()

    def left(unit, value):
        even = jnp.concatenate([value[:, 256 * i : 256 * i + 128] for i in range(4)], 1)
        odd = jnp.concatenate([value[:, 256 * i + 128 : 256 * i + 256] for i in range(4)], 1)
        at = pl.ds(512 * unit, 512) if isinstance(unit, int) else pl.ds(pl.multiple_of(512 * unit, 512), 512)

        @pl.when(core == 0)
        def _():
            mine_ref[:, at] = even
            theirs_ref[:, at] = odd

        @pl.when(core == 1)
        def _():
            mine_ref[:, at] = odd
            theirs_ref[:, at] = even

    low_lanes = iota((ROWS, SIZE), 1) < 64
    moves.need()
    for i in range(8):
        a, b = mixed_ref[2 * i].astype(F32), mixed_ref[2 * i + 1].astype(F32)
        at = slice(128 * i, 128 * i + 128)
        half[0, :, at] = jnp.where(low_lanes, a, swap_halves(b)).astype(BF16)
        half[1, :, at] = jnp.where(low_lanes, swap_halves(a), b).astype(BF16)
    out_ref[...] = x_ref[...]
    for t in range(2):
        left(t, half[t])
        copies[t].wait()
        out_ref[...] += matmul(half[t], w[t])
    middle = out_ref[...]
    scale = mean_scale(middle)
    normal[...] = middle * scale
    normal_low = normal[...].astype(BF16)
    left(2, normal_low)
    live = iota((ROWS, 1), 0) < count
    branch = jnp.where(live, cot_ref[...], 0.0).astype(BF16)
    right_ref[:, 7 * WIDTH :] = branch
    mg_ref[...] = jnp.zeros_like(mg_ref)
    for t in range(3):
        copies[2 + t].wait()
        copies[5 + t].wait()
        copies[8 + t].wait()
        gate[...] = matmul(normal_low, w[2 + t])
        up[...] = matmul(normal_low, w[5 + t])
        g, u = gate[...], up[...]
        sig = 1.0 / (1.0 + jnp.exp(-g))
        inner = (g * sig * u).astype(BF16)
        left(3 + t, inner)
        out_ref[...] += matmul(inner, w[8 + t])
        grad_inner = matmul_nt(branch, w[8 + t])
        gate_grad = (grad_inner * u * sig * (1.0 + g * (1.0 - sig))).astype(BF16)
        up_grad = (grad_inner * g * sig).astype(BF16)
        right_ref[:, WIDTH * (1 + t) : WIDTH * (2 + t)] = gate_grad
        right_ref[:, WIDTH * (4 + t) : WIDTH * (5 + t)] = up_grad
        mg_ref[...] += matmul_nt(gate_grad, w[2 + t])
        mg_ref[...] += matmul_nt(up_grad, w[5 + t])
    middle_grad = jnp.where(live, cot_ref[...], 0.0) + norm_back(mg_ref[...], normal[...], scale)
    mg_ref[...] = middle_grad
    attn_grad = middle_grad.astype(BF16)
    right_ref[:, :WIDTH] = attn_grad
    first = matmul_nt(attn_grad, w[0])
    second = matmul_nt(attn_grad, w[1])
    for i in range(8):
        a, b = first[:, 128 * i : 128 * i + 128], second[:, 128 * i : 128 * i + 128]
        send_ref[2 * i] = jnp.where(low_lanes, a, swap_halves(b)).astype(BF16)
        send_ref[2 * i + 1] = jnp.where(low_lanes, swap_halves(a), b).astype(BF16)


def feed(scal, mixed, x, cotangent, ff):
    outs = [
        ((ROWS, WIDTH), F32),
        ((ROWS, WIDTH), F32),
        ((HEADS, ROWS, SIZE), BF16),
        ((ROWS, 3072), BF16),
        ((ROWS, 3072), BF16),
        ((ROWS, 8 * WIDTH), BF16),
    ]
    scratch = [
        pltpu.VMEM((UNITS, WIDTH, WIDTH), BF16),
        pltpu.SemaphoreType.DMA((UNITS,)),
        pltpu.VMEM((ROWS, WIDTH), F32),
        pltpu.VMEM((ROWS, WIDTH), F32),
        pltpu.VMEM((2, ROWS, WIDTH), BF16),
        pltpu.VMEM((ROWS, WIDTH), F32),
    ]
    return call(
        feed_kernel, outs, (scal, mixed, x, cotangent, ff), (0,), (4,), scratch=scratch,
        flops=6 * 10**9, nbytes=28 * MIB,
    )


def weigh_kernel(moves, scal, lm_ref, lt_ref, rm_ref, rt_ref, after, *refs):
    outs, (left, right), buffers = refs[:8], refs[8:10], refs[10:]
    moves.need(1, 2)
    for l in range(6):
        at = slice(512 * l, 512 * l + 512)
        left[at, :128] = lm_ref[:, at].astype(F32).T.astype(BF16)
        left[at, 128:] = lt_ref[:, at].astype(F32).T.astype(BF16)
    moves.need()
    right[:128] = rm_ref[...]
    right[128:] = rt_ref[...]
    for s, (part, mode, halves) in enumerate(QUARTERS):
        buffer = buffers[s]
        for n, (unit, c) in enumerate(halves):
            l, r = PAIRS[unit]
            at = WIDTH * r + 512 * c
            out = matmul(left[512 * l : 512 * l + 512], right[:, at : at + 512])
            for i in range(4):
                if part == 0:
                    block = out[128 * i : 128 * i + 128]
                else:
                    rows = [128 * x + 32 * i for x in range(4)]
                    block = jnp.concatenate([out[r : r + 32] for r in rows], 0)
                buffer[i, n] = block.astype(BF16)
        for i, mask in enumerate(KEPT[mode]):
            moves.push(buffer.at[scal[part] ^ mask], outs[2 * s + i // 2].at[i % 2])


def weigh(scal, mine, theirs, right, right_theirs, after):
    outs = [((2, len(h), 128, 512), BF16) for p, m, h in QUARTERS for i in range(2)]
    scratch = [pltpu.VMEM((3072, 256), BF16), pltpu.VMEM((256, 8 * WIDTH), BF16)]
    scratch += [pltpu.VMEM((4, len(h), 128, 512), BF16) for p, m, h in QUARTERS]
    out = call(
        weigh_kernel, outs, (scal, mine, theirs, right, right_theirs, after), (0,), (5,), range(8),
        scratch, flops=3 * 10**9, nbytes=18 * MIB, sends=16,
    )
    return out[::2], out[1::2]


AXES = ("x", "y", "z")


def add(a, b):
    return a.astype(F32) + b.astype(F32)


def four(refs):
    return add(refs[0][...], refs[1][...]) + add(refs[2][...], refs[3][...])


def add_first_kernel(moves, *refs):
    keeps, gots, (after,), new_keeps, new_sends = refs[:4], refs[4:8], refs[8:9], refs[9:13], refs[13:]
    for s in range(4):
        moves.need(s, 4 + s)
        new_sends[s][...] = add(keeps[s][1], gots[s][1]).astype(BF16)
        moves.flush(4 + s)
        new_keeps[s][...] = add(keeps[s][0], gots[s][0]).astype(BF16)
        moves.flush(s)


def add_first(keeps, gots, after):
    outs = [(k.shape[1:], BF16) for k in keeps] * 2
    out = call(
        add_first_kernel, outs, (*keeps, *gots, after), anywhere=(8,), flops=10**7, nbytes=17 * MIB
    )
    return out[:4], out[4:]


PART_ROWS = 32 * len(PARTS[0])


def join_kernel(moves, scal, *refs):
    keeps, gots, (mine_ref, theirs_ref), outs, buffers = refs[:4], refs[4:8], refs[8:10], refs[10:18], refs[18:]
    for s, (part, mode, halves) in enumerate(QUARTERS):
        moves.need(1 + s, 5 + s)
        first = 32 * 6 * mode
        for n in range(len(halves)):
            total = add(keeps[s][n], gots[s][n])
            for i in range(4):
                at = first + 32 * n
                buffers[part][i, at : at + 32] = total[32 * i : 32 * i + 32].astype(BF16)
        if s == 1:
            for mask in range(4):
                moves.push(buffers[0].at[scal[1] ^ mask], outs[mask])
    moves.need()
    for x in range(4):
        buffers[1][x, PART_ROWS:] = add(mine_ref[x], theirs_ref[x]).astype(BF16)
    for mask in range(4):
        moves.push(buffers[1].at[scal[0] ^ mask], outs[4 + mask])


def join(scal, keeps, gots, mine, theirs):
    shapes = [(PART_ROWS, 512), (PART_ROWS + ROWS, 512)]
    outs = [(shape, BF16) for shape in shapes for mask in range(4)]
    scratch = [pltpu.VMEM((4, *shape), BF16) for shape in shapes]
    return call(
        join_kernel, outs, (scal, *keeps, *gots, mine, theirs), (0,), (), range(8), scratch,
        flops=10**7, nbytes=10 * MIB, sends=8,
    )


def pass_on_kernel(moves, scal, *refs):
    got, outs, heads_ref, buffer = refs[:8], refs[8:12], refs[12], refs[13]
    for part in (1, 0):
        moves.need(*range(1 + 4 * part, 5 + 4 * part))
        total = four(got[4 * part : 4 * part + 4])
        if part == 1:
            for f in range(HEADS):
                at = PART_ROWS + 8 * f
                heads_ref[f] = total[at : at + 8].astype(BF16)
            moves.flush(4)
        for n in range(11):
            for i in range(4):
                at = 88 * part + 8 * n
                buffer[i, at : at + 8] = total[32 * n + 8 * i : 32 * n + 8 * i + 8].astype(BF16)
    for mask in range(4):
        moves.push(buffer.at[scal[2] ^ mask], outs[mask])


def pass_on(scal, got):
    outs = [((176, 512), BF16)] * 4 + [((HEADS, 8, 512), BF16)]
    out = call(
        pass_on_kernel, outs, (scal, *got), (0,), raw=range(4),
        scratch=[pltpu.VMEM((4, 176, 512), BF16)], flops=10**7, nbytes=5 * MIB, sends=4,
    )
    return out[:4], out[4]


def finish_heads_kernel(
    moves, back_ref, q_ref, k_ref, v_ref, g1_ref, dq_ref, dk_ref, dv_ref, dg_ref, dqk_ref
):
    moves.need()
    gain = column(g1_ref[...].astype(BF16).astype(F32))
    order = channel_map(True)
    dg = jnp.zeros((8, 1), F32)
    extra = jnp.zeros((8, SIZE), F32)
    for h in range(KV_HEADS):
        pair = []
        for f in (2 * h, 2 * h + 1):
            total = back_ref[f].astype(F32)
            at = slice(128 * f, 128 * f + 128)
            dq_ref[0, :, at] = total[:, :128] * gain
            w = q_ref[0, :, at].astype(BF16).astype(F32)
            dg += jnp.sum(total[:, :128] * w, 1, keepdims=True)
            extra += total[:, 384:]
            pair.append(total)
        at = slice(128 * h, 128 * h + 128)
        both = pair[0] + pair[1]
        dk = both[:, 128:256]
        dv = exact(both[:, 256:384], order)
        dk_ref[0, :, at] = dk * gain
        dv_ref[0, :, at] = dv * gain
        dg += jnp.sum(dk * k_ref[0, :, at].astype(BF16).astype(F32), 1, keepdims=True)
        dg += jnp.sum(dv * v_ref[0, :, at].astype(BF16).astype(F32), 1, keepdims=True)
    dg_ref[...] = jnp.sum(jnp.where(iota((8, 8), 0) == iota((8, 8), 1), dg, 0.0), 0, keepdims=True)
    dqk_ref[...] = jnp.broadcast_to(jnp.sum(extra, 1, keepdims=True), (8, SIZE))


def finish_heads(back, q, k, v, g1):
    outs = [((1, 8, 2048), F32), ((1, 8, 1024), F32), ((1, 8, 1024), F32), ((1, 8), F32), ((8, SIZE), F32)]
    return call(finish_heads_kernel, outs, (back, q, k, v, g1), flops=10**7, nbytes=3 * MIB)


def finish_feed_kernel(moves, *refs):
    got, (g_ref, u_ref, g2_ref), outs = refs[:4], refs[4:7], refs[7:]
    do_ref, dg_ref, du_ref, dd_ref, gain_ref = outs
    moves.need()
    total = four(got)
    tiles = {key: total[8 * n : 8 * n + 8] for n, key in enumerate(HALVES)}
    units = [jnp.concatenate([tiles[u, 0], tiles[u, 1]], 1) for u in range(UNITS)]
    for t in range(2):
        do_ref[0, 8 * t : 8 * t + 8] = units[t]
    for t in range(3):
        dd_ref[0, 8 * t : 8 * t + 8] = units[8 + t]
    gain = column(g2_ref[...].astype(BF16).astype(F32))
    order = hidden_map(True)
    dg = jnp.zeros((8, 1), F32)
    for base, w_ref, out_ref in ((2, g_ref, dg_ref), (5, u_ref, du_ref)):
        tall = jnp.concatenate(
            [
                jnp.concatenate([units[base + t][:, 128 * i : 128 * i + 128] for t in range(3)], 1)
                for i in range(8)
            ],
            0,
        )
        tall = exact(tall, order)
        for i in range(8):
            at = slice(384 * i, 384 * i + 384)
            grad = tall[8 * i : 8 * i + 8]
            dg += jnp.sum(grad * w_ref[0, :, at].astype(BF16).astype(F32), 1, keepdims=True)
            out_ref[0, :, at] = grad * gain
    gain_ref[...] = jnp.sum(jnp.where(iota((8, 8), 0) == iota((8, 8), 1), dg, 0.0), 0, keepdims=True)


def finish_feed(got, gate, up, g2):
    outs = [
        ((1, 16, 1024), F32), ((1, 8, 3072), F32), ((1, 8, 3072), F32), ((1, 24, 1024), F32), ((1, 8), F32),
    ]
    return call(finish_feed_kernel, outs, (*got, gate, up, g2), flops=10**8, nbytes=3 * MIB)


def finish_input_kernel(moves, low_ref, w_ref, x_ref, mg_ref, out_ref):
    moves.need(0)
    halves = [
        jnp.concatenate([low_ref[8 * i + h, :, :128] for h in range(8)], 1) for i in range(2)
    ]
    for at in (slice(128, 256), slice(256, 384)):
        pairs = [add(low_ref[2 * h, :, at], low_ref[2 * h + 1, :, at]) for h in range(8)]
        halves.append(jnp.concatenate(pairs, 1).astype(BF16))
    moves.need(1)
    out_ref[...] = matmul_nt(halves[0], w_ref[0])
    for i in range(1, 4):
        out_ref[...] += matmul_nt(halves[i], w_ref[i])
    moves.need()
    x = x_ref[...]
    scale = mean_scale(x)
    out_ref[...] = mg_ref[...] + norm_back(out_ref[...], x * scale, scale)


def finish_input(low, weights, x, middle_grad):
    return call(
        finish_input_kernel, [((ROWS, WIDTH), F32)], (low, weights, x, middle_grad),
        flops=10**9, nbytes=11 * MIB,
    )[0]


def other(v):
    return lax.ppermute(v, "core", [(0, 1), (1, 0)])


def trade(v, axes):
    return lax.all_to_all(v, axes, split_axis=0, concat_axis=0, tiled=True)


def swap(terms, axis):
    return [terms[0]] + [
        lax.ppermute(terms[mask], axis, [(i, i ^ mask) for i in range(4)]) for mask in (1, 3, 2)
    ]


def in_order(v):
    return [v[0], v[1], v[3], v[2]]


def shards(
    block_input, counts, query_weight, key_matrix, value_matrix, out_weight, gate_weight,
    up_weight, down_weight, attn_gain, mlp_gain, query_gain, key_gain, cotangent,
):
    place = lax.axis_index(TOKENS)
    group = lax.axis_index(("x", "core"))
    core = lax.axis_index("core")
    own = lax.axis_index(ALL).reshape(1).astype(jnp.int32)
    ff_pack, early, late = prepare(
        block_input, out_weight, gate_weight, up_weight, down_weight, mlp_gain
    )
    ff = lax.all_gather(ff_pack, ALL, axis=1, tiled=True)
    blocks = [swap([early] * 4, "y"), swap([late] * 4, "z")]
    head_send = pack_heads(
        own, query_gain, key_gain, query_weight, key_matrix, value_matrix, attn_gain, ff_pack
    )
    head_weights = jnp.stack(in_order(swap([trade(head_send, TOKENS).reshape(ROWS, 512)] * 4, "x")))
    head_weights = (head_weights, other(head_weights))
    blocks = [jnp.stack(in_order(b)) for b in blocks]
    tokens = []
    for block, axis in zip(blocks, "zy"):
        tokens += in_order(swap([block] * 4, axis))

    group_counts = lax.dynamic_index_in_dim(counts, group, 0, keepdims=False)
    starts = jnp.cumsum(group_counts) - group_counts
    own_count = lax.dynamic_index_in_dim(group_counts, place, 0, keepdims=False)
    scal = jnp.concatenate(
        [place.reshape(1), jnp.sum(group_counts).reshape(1), starts, group_counts]
        + [lax.axis_index(a).reshape(1) for a in ("y", "z", "x", "core")]
    ).astype(jnp.int32)
    inverse = ROPE_BASE ** (-(jnp.arange(64, dtype=F32) * 2.0 / SIZE))
    position = starts[:, None] + jnp.arange(ROWS, dtype=jnp.int32)[None, :]
    angles = position.astype(F32)[:, :, None] * inverse
    cosine, sine = jnp.cos(angles), jnp.sin(angles)
    cos = jnp.concatenate([cosine, cosine], -1)
    sin = jnp.concatenate([-sine, sine], -1)

    mixed_head, *saved, projected, head_weight = attend(scal, tokens, head_weights, cos, sin)
    rows = pack_rows(query_weight, key_matrix, value_matrix, attn_gain, mixed_head)
    rows = lax.all_gather(rows, ALL, axis=1, tiled=True)
    mixed = trade(mixed_head, TOKENS)
    block_output, middle_grad, grad_send, mine, theirs, right = feed(
        jnp.stack([core, own_count]).astype(jnp.int32), mixed, block_input, cotangent, ff
    )
    head_grad = trade(grad_send, TOKENS)

    chip = jnp.stack([lax.axis_index(a) for a in AXES]).astype(jnp.int32)
    keeps, sends = weigh(chip, mine, other(theirs), right, other(right), head_grad)

    def step(sends, order):
        return [
            lax.ppermute(v, ORDERS[part][0], [(i, i ^ MASKS[mode][order]) for i in range(4)])
            for v, (part, mode, halves) in zip(sends, QUARTERS)
        ]

    gots = step(sends, 0)
    grads = retreat(scal, head_grad, [mixed_head] + saved, sends[0])
    keeps, sends = add_first(keeps, gots, grads[0])
    gots = step(sends, 1)
    low, head_gains = project(scal, head_weight, cos, sin, projected, grads, sends[0])
    token_low = trade(low, TOKENS)
    head_mine, head_theirs = weigh_heads(scal, tokens, low, head_gains)
    terms = join(chip, keeps, gots, head_mine, other(head_theirs))
    terms, head_terms = pass_on(chip, swap(terms[:4], "y") + swap(terms[4:], "x"))
    got = swap(terms, "z")
    head_back = trade(head_terms, TOKENS)
    input_grad = finish_input(token_low, rows, block_input, middle_grad)
    query_grad, key_grad, value_grad, attn_gain_grad, head_gains = finish_heads(
        head_back, query_weight, key_matrix, value_matrix, attn_gain
    )
    out_grad, gate_grad, up_grad, down_grad, mlp_gain_grad = finish_feed(
        got, gate_weight, up_weight, mlp_gain
    )
    return (
        block_output,
        input_grad,
        query_grad,
        key_grad,
        value_grad,
        out_grad,
        gate_grad,
        up_grad,
        down_grad,
        attn_gain_grad,
        mlp_gain_grad,
        head_gains[0:1, 0:1],
        head_gains[1:2, 0:1],
    )


def solution(mesh):
    fine = Mesh(mesh.devices.reshape(4, 2, 4, 4), ALL)
    tokens = P(ALL, None)
    weight = P(None, ALL, None)
    gain = P(None, ALL)
    return jax.shard_map(
        shards,
        mesh=fine,
        in_specs=(tokens, P()) + (weight,) * 7 + (gain,) * 4 + (tokens,),
        out_specs=(tokens, tokens) + (weight,) * 7 + (gain,) * 4,
        check_vma=False,
    )
```

time: 4120 us -> 365 us (0.09)
  waiting for transfers between devices: 3670 us -> 124 us
  matrix products: 151 us -> 0 us
  blocking collectives: 135 us -> 12.1 us
  Pallas kernels: 0 us -> 116 us
  starting transfers between devices: 1.51 us -> 69 us
  local copies, waits for them, and re-layouts: 75.9 us -> 11.2 us
  other arithmetic: 56 us -> 10.2 us
    reduce_scatter x9 -> x0, waiting for transfers between devices: 3270 us -> none  [the longest x1 648 us: shards(): lax.psum_scatter(layer_grads[3], ('dp', 'fsdp'), scatter_dimension=0, til...]
    all_gather x9 -> x2, waiting for transfers between devices: 397 us -> 10.1 us  [the longest x1 10.1 us: shards(): ff = lax.all_gather(ff_pack, ALL, axis=1, tiled=True)]
    dot_general x49 -> x0, matrix products: 151 us -> none  [the longest x8 24.1 us: score_block(): jnp.einsum('rhgd,khd->hgrk', query_rows, key_block, preferred_element_typ...]
    unnamed x2 -> x0, blocking collectives: 135 us -> none
    pallas_call x0 -> x15, Pallas kernels: none -> 116 us  [call(): pl.pallas_call(body, out_shape=[jax.ShapeDtypeStruct(s, t) for s, t in ou...]
    ppermute x0 -> x36, waiting for transfers between devices: none -> 87.6 us  [the longest x24 60.6 us: swap(): lax.ppermute(terms[mask], axis, [(i, i ^ mask) for i in range(4)])]
    ppermute x0 -> x36, starting transfers between devices: none -> 47.3 us  [the longest x24 35.3 us: swap(): lax.ppermute(terms[mask], axis, [(i, i ^ mask) for i in range(4)])]
  transfers between devices with their start and end apart: 18 -> 42, of which waited for: 17 -> 20; matrix products, arithmetic and copies ran while one was open for 4% -> 4% of each run, Pallas kernels for 0% -> 30%
where the time goes in v1:
time: 365 us; the launch traced here: 359 us
  waiting for transfers between devices  124 us (34%)
  Pallas kernels  116 us (32%)
  starting transfers between devices  69 us (19%)
  between operations  16.3 us (4%)
  blocking collectives  12.1 us (3%)
  local copies, waits for them, and re-layouts  11.2 us (3%)
  other arithmetic  10.2 us (3%)
    pallas_call x15, Pallas kernels, call(): pl.pallas_call(body, out_shape=[jax.ShapeDtypeStruct(s, t) for s, t in ou...  116 us
    ppermute x24, waiting for transfers between devices, swap(): lax.ppermute(terms[mask], axis, [(i, i ^ mask) for i in range(4)])  60.6 us
    ppermute x24, starting transfers between devices, swap(): lax.ppermute(terms[mask], axis, [(i, i ^ mask) for i in range(4)])  35.3 us
    all_to_all x4, waiting for transfers between devices, trade(): return lax.all_to_all(v, axes, split_axis=0, concat_axis=0, tiled=True)  26.4 us
    ppermute x8, waiting for transfers between devices, step(): lax.ppermute(v, ORDERS[part][0], [(i, i ^ MASKS[mode][order]) for i in ra...  24.8 us
    all_to_all x4, starting transfers between devices, trade(): return lax.all_to_all(v, axes, split_axis=0, concat_axis=0, tiled=True)  21.7 us
    all_to_all x1, blocking collectives, trade(): return lax.all_to_all(v, axes, split_axis=0, concat_axis=0, tiled=True)  12.1 us
    ppermute x8, starting transfers between devices, step(): lax.ppermute(v, ORDERS[part][0], [(i, i ^ MASKS[mode][order]) for i in ra...  11.1 us
  transfers between devices with their start and end apart: 42, of which 20 were waited for; matrix products, arithmetic and copies ran while one was open for 4% of the time, Pallas kernels for 30%

profile of v1, /device:TPU:0, one launch (start us, length us, event | category | flops | bytes accessed | tf_op | source)
XLA Modules:
  0.0 359.2 jit_solution(17537232208715683752)
XLA Ops:
  9.7 4.2 %collective-permute-start.8 = (bf16[128,512]{1,0:T(8,128)(2,1)}, bf16[128,512]{1,0:T(8,128)(2,1)S(1)}, u32[]{:S(2)}, u32[]{:S(2)}) collective-permute-start(bf16[128,512]{1,0:T(8,128)(2,1)} %get-tuple-element.76), channel_id=1, source_target_pairs={{0,3},{1,2},{2,1},{3,0},{4,7},{5,6},{6,5},{7,4},{8,11},{9,10},{10,... | collective-permute-start | bytes 393224 | tf_op jit(solution)/shard_map/ppermute | solution.py:826
  21.6 6.9 %all-to-all-start = ((bf16[16,8,512]{2,1,0:T(8,128)(2,1)}), bf16[16,8,512]{2,1,0:T(8,128)(2,1)S(1)}, u32[]{:S(2)}, u32[]{:S(2)}) async-start(bf16[16,8,512]{2,1,0:T(8,128)(2,1)} %shard_map.238), calls=%async_computation | async-start | bytes 262144 | tf_op jit(solution)/shard_map/all_to_all | solution.py:821
  48.9 12.7 %collective-permute-done.11.refs_8_ = bf16[4,128,512]{2,1,0:T(8,128)(2,1)S(1)} collective-permute-done((bf16[4,128,512]{2,1,0:T(8,128)(2,1)S(1)}, bf16[4,128,512]{2,1,0:T(8,128)(2,1)S(1)}, u32[]{:S(2)}, u32[]{:S(2)}) %collective-permute-start.11) | collective-permute-done | bytes 524320 | tf_op jit(solution)/shard_map/ppermute | solution.py:826
  70.2 4.9 %collective-permute-done.5.refs_4_ = bf16[4,128,512]{2,1,0:T(8,128)(2,1)} collective-permute-done((bf16[4,128,512]{2,1,0:T(8,128)(2,1)S(1)}, bf16[4,128,512]{2,1,0:T(8,128)(2,1)}, u32[]{:S(2)}, u32[]{:S(2)}) %collective-permute-start.5) | collective-permute-done | bytes 524320 | tf_op jit(solution)/shard_map/ppermute | solution.py:826
  76.2 18.1 %shard_map.239 = (bf16[16,128,128]{2,1,0:T(8,128)(2,1)}, bf16[16,128,128]{2,1,0:T(8,128)(2,1)}, bf16[2048,128]{1,0:T(8,128)(2,1)}, bf16[2048,128]{1,0:T(8,128)(2...) custom-call(s32[38]{0:T(128)} %concatenate.9.refs_0_, bf16[4,128,512]{2,1,0:T(8,128)(2,1)} %copy-done.9, ...), custom_call_target="tpu_custom_call" | custom-call | flops 5000000000 | bytes 12582912 | tf_op jit(solution)/shard_map/pallas_call | solution.py:117
  96.1 5.7 %all-to-all-start.1 = ((bf16[16,128,128]{2,1,0:T(8,128)(2,1)}), bf16[16,128,128]{2,1,0:T(8,128)(2,1)S(1)}, u32[]{:S(2)}, u32[]{:S(2)}) async-start(bf16[16,128,128]{2,1,0:T(8,128)(2,1)} %get-tuple-element.78.refs_2_.refs_4_), calls=%async_computation.1 | async-start | bytes 1048576 | tf_op jit(solution)/shard_map/all_to_all | solution.py:821
  104.3 12.7 %all-to-all-done.1.refs_1_ = bf16[16,128,128]{2,1,0:T(8,128)(2,1)S(1)} async-done(((bf16[16,128,128]{2,1,0:T(8,128)(2,1)}), bf16[16,128,128]{2,1,0:T(8,128)(2,1)S(1)}, u32[]{:S(2)}, u32[]{:S(2)}) %all-to-all-start.1) | async-done | bytes 524320 | tf_op jit(solution)/shard_map/all_to_all | solution.py:821
  117.0 10.1 %all-gather.3.cloned.1.call-done.refs_4_ = bf16[11,1024,1024]{2,1,0:T(8,128)(2,1)} async-done(((bf16[11,8,1024]{2,1,0:T(8,128)(2,1)}), bf16[11,1024,1024]{2,1,0:T(8,128)(2,1)}) %all-gather.3.cloned.1.call-update) | async-done | bytes 23068688 | tf_op jit(solution)/shard_map/all_gather | solution.py:845
  127.2 23.0 %shard_map.240 = (f32[128,1024]{1,0:T(8,128)}, f32[128,1024]{1,0:T(8,128)}, bf16[16,128,128]{2,1,0:T(8,128)(2,1)}, bf16[128,3072]{1,0:T(8,128)(2,1)}, bf16[128,3...) custom-call(s32[2]{0:T(128)} %pad_add_fusion.refs_0_, bf16[16,128,128]{2,1,0:T(8,128)(2,1)} %copy-done.1, f32[128,1024]{1,0:T(8,128)} %refs_2_.9, ...), custom_call_target="tpu_custom_call" | custom-call | flops 6000000000 | bytes 29360128 | tf_op jit(solution)/shard_map/pallas_call | solution.py:117
  150.7 5.2 %all-to-all-start.2 = ((bf16[16,128,128]{2,1,0:T(8,128)(2,1)}), bf16[16,128,128]{2,1,0:T(8,128)(2,1)S(1)}, u32[]{:S(2)}, u32[]{:S(2)}) async-start(bf16[16,128,128]{2,1,0:T(8,128)(2,1)} %get-tuple-element.82), calls=%async_computation.2 | async-start | bytes 1048576 | tf_op jit(solution)/shard_map/all_to_all | solution.py:821
  156.5 12.4 %all-to-all-done.2.refs_5_.refs_1_ = bf16[16,128,128]{2,1,0:T(8,128)(2,1)S(1)} async-done(((bf16[16,128,128]{2,1,0:T(8,128)(2,1)}), bf16[16,128,128]{2,1,0:T(8,128)(2,1)S(1)}, u32[]{:S(2)}, u32[]{:S(2)}) %all-to-all-start.2) | async-done | bytes 524320 | tf_op jit(solution)/shard_map/all_to_all | solution.py:821
  170.7 8.8 %shard_map.241 = (bf16[2,6,128,512]{3,2,1,0:T(8,128)(2,1)}, bf16[2,6,128,512]{3,2,1,0:T(8,128)(2,1)}, bf16[2,5,128,512]{3,2,1,0:T(8,128)(2,1)}, bf16[2,5,128,512...) custom-call(s32[3]{0:T(128)} %pad_add_fusion.1.refs_0_, ...), custom_call_target="tpu_custom_call" | custom-call | flops 3000000000 | bytes 18874368 | tf_op jit(solution)/shard_map/pallas_call | solution.py:117
  184.7 15.2 %shard_map.242 = (f32[4,512,128]{2,1,0:T(8,128)}, f32[2176,128]{1,0:T(8,128)}, f32[2176,128]{1,0:T(8,128)}) custom-call(s32[38]{0:T(128)} %concatenate.9.refs_0_, bf16[16,128,128]{2,1,0:T(8,128)(2,1)} %copy-done.11, bf16[16,128,128]{2,1,0:T(8,128)(2,1)} %get-tuple-element.78.refs_2_.refs_4_, bf16[16,128,128]{2,1,0:T(8,128)(2,1)} %get-tuple-element.83.refs_3_, ...), custom_call_target="tpu_custom_call" | custom-call | flops 8000000000 | bytes 6291456 | tf_op jit(solution)/shard_map/pallas_call | solution.py:117
  199.8 21.7 %collective-permute-done.19.refs_5_ = bf16[2,5,128,512]{3,2,1,0:T(8,128)(2,1)} collective-permute-done((bf16[2,5,128,512]{3,2,1,0:T(8,128)(2,1)}, bf16[2,5,128,512]{3,2,1,0:T(8,128)(2,1)}, u32[]{:S(2)}, u32[]{:S(2)}) %collective-permute-start.19) | collective-permute-done | bytes 1310752 | tf_op jit(solution)/shard_map/ppermute | solution.py:885
  225.8 6.1 %shard_map.243 = (bf16[6,128,512]{2,1,0:T(8,128)(2,1)}, bf16[5,128,512]{2,1,0:T(8,128)(2,1)}, bf16[6,128,512]{2,1,0:T(8,128)(2,1)}, bf16[5,128,512]{2,1,0:T(8,12...) custom-call(bf16[2,6,128,512]{3,2,1,0:T(8,128)(2,1)} %get-tuple-elem, ...), custom_call_target="tpu_custom_call" | custom-call | flops 10000000 | bytes 17825792 | tf_op jit(solution)/shard_map/pallas_call | solution.py:117
  237.9 9.9 %shard_map.244 = (bf16[16,128,384]{2,1,0:T(8,128)(2,1)}, f32[8,128]{1,0:T(8,128)}) custom-call(s32[38]{0:T(128)} %concatenate.9.refs_0_, bf16[1024,512]{1,0:T(8,128)(2,1)} %get-tuple-element.80.refs_1_, f32[16,128,128]{2,1,0:T(8,128)} %get-tuple-element.144.refs_11_.refs_2_, f32[16,128,128]{2,1,0:T(8,128)} %get-tuple-element.145.refs_12_.refs_3_, ...), custom_call_target="tpu_custom_call" | custom-call | flops 100000000 | bytes 10485760 | tf_op jit(solution)/shard_map/pallas_call | solution.py:117
  247.8 7.1 %shard_map.247 = (bf16[4,128,512]{2,1,0:T(8,128)(2,1)}, bf16[4,128,512]{2,1,0:T(8,128)(2,1)}) custom-call(s32[38]{0:T(128)} %concatenate.9.refs_0_, bf16[4,128,512]{2,1,0:T(8,128)(2,1)} %copy-done.9, bf16[4,128,512]{2,1,0:T(8,128)(2,1)} %collective-permute-done.3.refs_2_, bf16[4,128,512]{2,1,0:T(8,128)(2,1)} %collective-permute-done.4.refs_3_, ...), custom_call_target="tpu_custom_call" | custom-call | flops 2000000000 | bytes 7340032 | tf_op jit(solution)/shard_map/pallas_call | solution.py:117
  258.8 5.2 %shard_map.248 = (bf16[352,512]{1,0:T(8,128)(2,1)}, bf16[352,512]{1,0:T(8,128)(2,1)}, bf16[352,512]{1,0:T(8,128)(2,1)}, bf16[352,512]{1,0:T(8,128)(2,1)}, bf16[4...) custom-call(s32[3]{0:T(128)} %pad_add_fusion.1.refs_0_, ...), custom_call_target="tpu_custom_call" | custom-call | flops 10000000 | bytes 10485760 | tf_op jit(solution)/shard_map/pallas_call | solution.py:117
  270.7 4.1 %collective-permute-done.27.refs_2_ = bf16[352,512]{1,0:T(8,128)(2,1)S(1)} collective-permute-done((bf16[352,512]{1,0:T(8,128)(2,1)}, bf16[352,512]{1,0:T(8,128)(2,1)S(1)}, u32[]{:S(2)}, u32[]{:S(2)}) %collective-permute-start.27) | collective-permute-done | bytes 360480 | tf_op jit(solution)/shard_map/ppermute | solution.py:826
  276.7 11.4 %collective-permute-done.28.refs_3_ = bf16[352,512]{1,0:T(8,128)(2,1)S(1)} collective-permute-done((bf16[352,512]{1,0:T(8,128)(2,1)}, bf16[352,512]{1,0:T(8,128)(2,1)S(1)}, u32[]{:S(2)}, u32[]{:S(2)}) %collective-permute-start.28) | collective-permute-done | bytes 360480 | tf_op jit(solution)/shard_map/ppermute | solution.py:826
  292.9 4.0 %shard_map.249 = (bf16[176,512]{1,0:T(8,128)(2,1)}, bf16[176,512]{1,0:T(8,128)(2,1)}, bf16[176,512]{1,0:T(8,128)(2,1)}, bf16[176,512]{1,0:T(8,128)(2,1)}, bf16[16,8,512]{2,1,0:T(8,128)(2,1)}) custom-call(s32[3]{0:T(128)} %pad_add_fusion.1.refs_0_, bf16[352,512]{1,0:T(8,128)(2,1)} %get-tuple-element.114.refs_1_, bf16[352,512]{1,0:T(8,128)(2,1)} %copy-done.16, ...), custom_call_target="tpu_custom_call" | custom-call | flops 10000000 | bytes 5242880 | tf_op jit(solution)/shard_map/pallas_call | solution.py:117
  296.9 12.1 %all_to_all.25.refs_0_ = bf16[16,8,512]{2,1,0:T(8,128)(2,1)} all-to-all(bf16[16,8,512]{2,1,0:T(8,128)(2,1)} %get-tuple-element.122), channel_id=1, replica_groups=mesh['x'=4,'core'=2,'y'=4,'z'=4] {'y','z'}, dimensions={0} | all-to-all | bytes 262144 | tf_op jit(solution)/shard_map/all_to_all | solution.py:821
  321.2 15.4 %collective-permute-done.33.refs_1_ = bf16[176,512]{1,0:T(8,128)(2,1)S(1)} collective-permute-done((bf16[176,512]{1,0:T(8,128)(2,1)S(1)}, bf16[176,512]{1,0:T(8,128)(2,1)S(1)}, u32[]{:S(2)}, u32[]{:S(2)}) %collective-permute-start.33) | collective-permute-done | bytes 180256 | tf_op jit(solution)/shard_map/ppermute | solution.py:826
  344.0 7.8 %shard_map.246 = f32[128,1024]{1,0:T(8,128)} custom-call(bf16[16,128,384]{2,1,0:T(8,128)(2,1)} %copy-done, bf16[4,1024,1024]{2,1,0:T(8,128)(2,1)} %all-gather.5.cloned.1.call-done.refs_1_, f32[128,1024]{1,0:T(8,128)} %refs_2_.9, f32[128,1024]{1,0:T(8,128)} %get-tuple-element.103.refs_3_), custom_call_target="tpu_custom_call" | custom-call | flops 1000000000 | bytes 11534336 | tf_op jit(solution)/shard_map/pallas_call | solution.py:117
  (155 shorter events, 98.1 us)
Async XLA Ops:
  7.2 120.0 %all-gather.3.cloned.1.call-start = ((), (), s32[]{:S(2)}) async-start(), calls=%async_computation.5 | async-start | bytes 23248896 | tf_op jit(solution)/shard_map/all_gather | solution.py:845
  9.7 20.4 %collective-permute-start.8 = (bf16[128,512]{1,0:T(8,128)(2,1)}, bf16[128,512]{1,0:T(8,128)(2,1)S(1)}, u32[]{:S(2)}, u32[]{:S(2)}) collective-permute-start(bf16[128,512]{1,0:T(8,128)(2,1)} %get-tuple-element.76), channel_id=1, source_target_pairs={{0,3},{1,2},{2,1},{3,0},{4,7},{5,6},{6,5},{7,4},{8,11},{9,10},{10,... | collective-permute-start | bytes 393224 | tf_op jit(solution)/shard_map/ppermute | solution.py:826
  14.9 22.3 %collective-permute-start.2 = (bf16[128,512]{1,0:T(8,128)(2,1)}, bf16[128,512]{1,0:T(8,128)(2,1)S(1)}, u32[]{:S(2)}, u32[]{:S(2)}) collective-permute-start(bf16[128,512]{1,0:T(8,128)(2,1)} %get-tuple-element.75), channel_id=1, source_target_pairs={{0,12},{4,8},{8,4},{12,0},{1,13},{5,9},{9,5},{13,1},{2,14},{6,10},... | collective-permute-start | bytes 393224 | tf_op jit(solution)/shard_map/ppermute | solution.py:826
  17.9 22.0 %collective-permute-start.1 = (bf16[128,512]{1,0:T(8,128)(2,1)}, bf16[128,512]{1,0:T(8,128)(2,1)S(1)}, u32[]{:S(2)}, u32[]{:S(2)}) collective-permute-start(bf16[128,512]{1,0:T(8,128)(2,1)} %get-tuple-element.75), channel_id=1, source_target_pairs={{0,8},{4,12},{8,0},{12,4},{1,9},{5,13},{9,1},{13,5},{2,10},{6,14},... | collective-permute-start | bytes 393224 | tf_op jit(solution)/shard_map/ppermute | solution.py:826
  28.5 314.4 %all-gather.5.cloned.1.call-start = ((), (), s32[]{:S(2)}) async-start(), calls=%async_computation.6 | async-start | bytes 8454144 | tf_op jit(solution)/shard_map/all_gather | solution.py:873
  33.1 28.5 %collective-permute-start.11 = (bf16[4,128,512]{2,1,0:T(8,128)(2,1)S(1)}, bf16[4,128,512]{2,1,0:T(8,128)(2,1)S(1)}, u32[]{:S(2)}, u32[]{:S(2)}) collective-permute-start(bf16[4,128,512]{2,1,0:T(8,128)(2,1)S(1)} %pad_maximum_fusion.3.refs_5_), channel_id=1, source_target_pairs={{0,12},{4,8},{8,4},{12,0},{1,13},{5,9},{9,5},{13,1},{2,14},{6,10},... | collective-permute-start | bytes 1572872 | tf_op jit(solution)/shard_map/ppermute | solution.py:826
  35.2 27.8 %collective-permute-start.10 = (bf16[4,128,512]{2,1,0:T(8,128)(2,1)S(1)}, bf16[4,128,512]{2,1,0:T(8,128)(2,1)S(1)}, u32[]{:S(2)}, u32[]{:S(2)}) collective-permute-start(bf16[4,128,512]{2,1,0:T(8,128)(2,1)S(1)} %pad_maximum_fusion.3.refs_5_), channel_id=1, source_target_pairs={{0,8},{4,12},{8,0},{12,4},{1,9},{5,13},{9,1},{13,5},{2,10},{6,14},... | collective-permute-start | bytes 1572872 | tf_op jit(solution)/shard_map/ppermute | solution.py:826
  43.8 26.4 %collective-permute-start.9 = (bf16[4,128,512]{2,1,0:T(8,128)(2,1)S(1)}, bf16[4,128,512]{2,1,0:T(8,128)(2,1)}, u32[]{:S(2)}, u32[]{:S(2)}) collective-permute-start(bf16[4,128,512]{2,1,0:T(8,128)(2,1)S(1)} %pad_maximum_fusion.3.refs_5_), channel_id=1, source_target_pairs={{0,4},{4,0},{8,12},{12,8},{1,5},{5,1},{9,13},{13,9},{2,6},{6,2},{1... | collective-permute-start | bytes 1572872 | tf_op jit(solution)/shard_map/ppermute | solution.py:826
  46.3 28.8 %collective-permute-start.5 = (bf16[4,128,512]{2,1,0:T(8,128)(2,1)S(1)}, bf16[4,128,512]{2,1,0:T(8,128)(2,1)}, u32[]{:S(2)}, u32[]{:S(2)}) collective-permute-start(bf16[4,128,512]{2,1,0:T(8,128)(2,1)S(1)} %pad_maximum_fusion.2.refs_1_), channel_id=1, source_target_pairs={{0,3},{1,2},{2,1},{3,0},{4,7},{5,6},{6,5},{7,4},{8,11},{9,10},{10,... | collective-permute-start | bytes 1572872 | tf_op jit(solution)/shard_map/ppermute | solution.py:826
  47.9 27.2 %collective-permute-start.4 = (bf16[4,128,512]{2,1,0:T(8,128)(2,1)S(1)}, bf16[4,128,512]{2,1,0:T(8,128)(2,1)}, u32[]{:S(2)}, u32[]{:S(2)}) collective-permute-start(bf16[4,128,512]{2,1,0:T(8,128)(2,1)S(1)} %pad_maximum_fusion.2.refs_1_), channel_id=1, source_target_pairs={{0,2},{1,3},{2,0},{3,1},{4,6},{5,7},{6,4},{7,5},{8,10},{9,11},{10,... | collective-permute-start | bytes 1572872 | tf_op jit(solution)/shard_map/ppermute | solution.py:826
  96.1 21.0 %all-to-all-start.1 = ((bf16[16,128,128]{2,1,0:T(8,128)(2,1)}), bf16[16,128,128]{2,1,0:T(8,128)(2,1)S(1)}, u32[]{:S(2)}, u32[]{:S(2)}) async-start(bf16[16,128,128]{2,1,0:T(8,128)(2,1)} %get-tuple-element.78.refs_2_.refs_4_), calls=%async_computation.1 | async-start | bytes 1048576 | tf_op jit(solution)/shard_map/all_to_all | solution.py:821
  179.5 44.4 %collective-permute-start.20 = (bf16[2,6,128,512]{3,2,1,0:T(8,128)(2,1)}, bf16[2,6,128,512]{3,2,1,0:T(8,128)(2,1)S(1)}, u32[]{:S(2)}, u32[]{:S(2)}) collective-permute-start(bf16[2,6,128,512]{3,2,1,0:T(8,128)(2,1)} %get-tuple-element.99), channel_id=1, source_target_pairs={{0,4},{4,0},{8,12},{12,8},{1,5},{5,1},{9,13},{13,9},{2,6},{6,2},{1... | collective-permute-start | bytes 4718600 | tf_op jit(solution)/shard_map/ppermute | solution.py:885
  179.6 45.0 %collective-permute-start.18 = (bf16[2,6,128,512]{3,2,1,0:T(8,128)(2,1)}, bf16[2,6,128,512]{3,2,1,0:T(8,128)(2,1)S(1)}, u32[]{:S(2)}, u32[]{:S(2)}) collective-permute-start(bf16[2,6,128,512]{3,2,1,0:T(8,128)(2,1)} %get-tuple-element.90.refs_7_), channel_id=1, source_target_pairs={{0,32},{32,0},{64,96},{96,64},{1,33},{33,1},{65,97},{97,65},{2,34}... | collective-permute-start | bytes 4718600 | tf_op jit(solution)/shard_map/ppermute | solution.py:885
  181.1 40.4 %collective-permute-start.19 = (bf16[2,5,128,512]{3,2,1,0:T(8,128)(2,1)}, bf16[2,5,128,512]{3,2,1,0:T(8,128)(2,1)}, u32[]{:S(2)}, u32[]{:S(2)}) collective-permute-start(bf16[2,5,128,512]{3,2,1,0:T(8,128)(2,1)} %get-tuple-element.98), channel_id=1, source_target_pairs={{0,96},{32,64},{64,32},{96,0},{1,97},{33,65},{65,33},{97,1},{2,98}... | collective-permute-start | bytes 3932168 | tf_op jit(solution)/shard_map/ppermute | solution.py:885
  183.2 40.1 %collective-permute-start.21 = (bf16[2,5,128,512]{3,2,1,0:T(8,128)(2,1)}, bf16[2,5,128,512]{3,2,1,0:T(8,128)(2,1)}, u32[]{:S(2)}, u32[]{:S(2)}) collective-permute-start(bf16[2,5,128,512]{3,2,1,0:T(8,128)(2,1)} %get-tuple-element.100), channel_id=1, source_target_pairs={{0,12},{4,8},{8,4},{12,0},{1,13},{5,9},{9,5},{13,1},{2,14},{6,10},... | collective-permute-start | bytes 3932168 | tf_op jit(solution)/shard_map/ppermute | solution.py:885
  231.9 25.2 %collective-permute-start.24 = (bf16[6,128,512]{2,1,0:T(8,128)(2,1)}, bf16[6,128,512]{2,1,0:T(8,128)(2,1)S(1)}, u32[]{:S(2)}, u32[]{:S(2)}) collective-permute-start(bf16[6,128,512]{2,1,0:T(8,128)(2,1)} %get-tuple-element.109), channel_id=1, source_target_pairs={{0,12},{4,8},{8,4},{12,0},{1,13},{5,9},{9,5},{13,1},{2,14},{6,10},... | collective-permute-start | bytes 2359304 | tf_op jit(solution)/shard_map/ppermute | solution.py:885
  234.1 23.1 %collective-permute-start.22 = (bf16[6,128,512]{2,1,0:T(8,128)(2,1)}, bf16[6,128,512]{2,1,0:T(8,128)(2,1)S(1)}, u32[]{:S(2)}, u32[]{:S(2)}) collective-permute-start(bf16[6,128,512]{2,1,0:T(8,128)(2,1)} %get-tuple-element.101.refs_8_), channel_id=1, source_target_pairs={{0,96},{32,64},{64,32},{96,0},{1,97},{33,65},{65,33},{97,1},{2,98}... | collective-permute-start | bytes 2359304 | tf_op jit(solution)/shard_map/ppermute | solution.py:885
  265.5 22.6 %collective-permute-start.30 = (bf16[480,512]{1,0:T(8,128)(2,1)}, bf16[480,512]{1,0:T(8,128)(2,1)S(1)}, u32[]{:S(2)}, u32[]{:S(2)}) collective-permute-start(bf16[480,512]{1,0:T(8,128)(2,1)} %get-tuple-element.119), channel_id=1, source_target_pairs={{0,32},{32,0},{64,96},{96,64},{1,33},{33,1},{65,97},{97,65},{2,34}... | collective-permute-start | bytes 1474568 | tf_op jit(solution)/shard_map/ppermute | solution.py:826
  267.2 24.7 %collective-permute-start.31 = (bf16[480,512]{1,0:T(8,128)(2,1)}, bf16[480,512]{1,0:T(8,128)(2,1)S(1)}, u32[]{:S(2)}, u32[]{:S(2)}) collective-permute-start(bf16[480,512]{1,0:T(8,128)(2,1)} %get-tuple-element.120), channel_id=1, source_target_pairs={{0,96},{32,64},{64,32},{96,0},{1,97},{33,65},{65,33},{97,1},{2,98}... | collective-permute-start | bytes 1474568 | tf_op jit(solution)/shard_map/ppermute | solution.py:826
  267.8 24.1 %collective-permute-start.32 = (bf16[480,512]{1,0:T(8,128)(2,1)}, bf16[480,512]{1,0:T(8,128)(2,1)S(1)}, u32[]{:S(2)}, u32[]{:S(2)}) collective-permute-start(bf16[480,512]{1,0:T(8,128)(2,1)} %get-tuple-element.121), channel_id=1, source_target_pairs={{0,64},{32,96},{64,0},{96,32},{1,65},{33,97},{65,1},{97,33},{2,66}... | collective-permute-start | bytes 1474568 | tf_op jit(solution)/shard_map/ppermute | solution.py:826
  308.9 33.9 %all-to-all-start.3 = ((bf16[16,128,384]{2,1,0:T(8,128)(2,1)}), bf16[16,128,384]{2,1,0:T(8,128)(2,1)S(1)}, u32[]{:S(2)}, u32[]{:S(2)}) async-start(bf16[16,128,384]{2,1,0:T(8,128)(2,1)} %get-tuple-element.102.refs_9_), calls=%async_computation.3 | async-start | bytes 3145728 | tf_op jit(solution)/shard_map/all_to_all | solution.py:821
  312.8 23.8 %collective-permute-start.33 = (bf16[176,512]{1,0:T(8,128)(2,1)S(1)}, bf16[176,512]{1,0:T(8,128)(2,1)S(1)}, u32[]{:S(2)}, u32[]{:S(2)}) collective-permute-start(bf16[176,512]{1,0:T(8,128)(2,1)S(1)} %copy-done.29), channel_id=1, source_target_pairs={{0,1},{1,0},{2,3},{3,2},{4,5},{5,4},{6,7},{7,6},{8,9},{9,8},{10,11... | collective-permute-start | bytes 540680 | tf_op jit(solution)/shard_map/ppermute | solution.py:826
  314.7 22.1 %collective-permute-start.34 = (bf16[176,512]{1,0:T(8,128)(2,1)S(1)}, bf16[176,512]{1,0:T(8,128)(2,1)S(1)}, u32[]{:S(2)}, u32[]{:S(2)}) collective-permute-start(bf16[176,512]{1,0:T(8,128)(2,1)S(1)} %copy-done.28), channel_id=1, source_target_pairs={{0,3},{1,2},{2,1},{3,0},{4,7},{5,6},{6,5},{7,4},{8,11},{9,10},{10,... | collective-permute-start | bytes 540680 | tf_op jit(solution)/shard_map/ppermute | solution.py:826
  316.8 22.4 %collective-permute-start.35 = (bf16[176,512]{1,0:T(8,128)(2,1)S(1)}, bf16[176,512]{1,0:T(8,128)(2,1)S(1)}, u32[]{:S(2)}, u32[]{:S(2)}) collective-permute-start(bf16[176,512]{1,0:T(8,128)(2,1)S(1)} %copy-done.27), channel_id=1, source_target_pairs={{0,2},{1,3},{2,0},{3,1},{4,6},{5,7},{6,4},{7,5},{8,10},{9,11},{10,... | collective-permute-start | bytes 540680 | tf_op jit(solution)/shard_map/ppermute | solution.py:826
  (48 other events, 453.2 us)
Sparse Core Ops, SparseCore 0:
  11.0 116.0 all-gather.2
  130.3 77.2 all-gather.4
